TPU v7x, 32 devices: a whole 2x2x4 slice. The times are simulated.
32 devices in a mesh: dp: 16 (over z, y, x), fsdp: 2 (over core).
Axes of the slice: x: 2, y: 2, z: 4, core: 2. Of those that a mesh axis runs over, the one named last changes fastest.
Arguments:
- tokens: bfloat16 [32, 256, 768], P(('dp', 'fsdp')), may hold values from -6 to 6
- lengths: int32 [32], P(('dp', 'fsdp')), may hold values from 64 to 256, as said below
- cotangent: bfloat16 [32, 256, 768], P(('dp', 'fsdp')), may hold values from -6 to 6
- gain: bfloat16 [768], P('fsdp'), may hold values from 0.5 to 1.5
- w_in: bfloat16 [768, 3072], P('fsdp'), may hold values from -0.21875 to 0.21875
- conv_w: bfloat16 [4, 1536], P(None, 'fsdp'), may hold values from -3 to 3
- conv_b: bfloat16 [1536], P('fsdp'), may hold values from -1.5 to 1.5
- w_x: bfloat16 [1536, 80], P('fsdp'), may hold values from -0.15625 to 0.15625
- w_dt: bfloat16 [48, 1536], P(None, 'fsdp'), may hold values from -0.875 to 0.875
- dt_bias: bfloat16 [1536], P('fsdp'), may hold values from -6.875 to -2.296875
- a_log: bfloat16 [16, 1536], P(None, 'fsdp'), may hold values from 0 to 2.765625
- d_skip: bfloat16 [1536], P('fsdp'), may hold values from 0.5 to 1.5
- w_out: bfloat16 [1536, 768], P('fsdp'), may hold values from -0.15625 to 0.15625
Outputs:
- output: bfloat16 [32, 256, 768], P(('dp', 'fsdp'))
- input_grad: float32 [32, 256, 768], P(('dp', 'fsdp'))
- grad_gain: float32 [768], P('fsdp')
- grad_in: float32 [768, 3072], P('fsdp')
- grad_conv_w: float32 [4, 1536], P(None, 'fsdp')
- grad_conv_b: float32 [1536], P('fsdp')
- grad_x: float32 [1536, 80], P('fsdp')
- grad_dt: float32 [48, 1536], P(None, 'fsdp')
- grad_dt_bias: float32 [1536], P('fsdp')
- grad_a_log: float32 [16, 1536], P(None, 'fsdp')
- grad_skip: float32 [1536], P('fsdp')
- grad_out: float32 [1536, 768], P('fsdp')
Inputs may be any that keep to these rules, and one draw needn't show every extreme that they name: A sequence's first lengths tokens are real and the rest padding; in every draw some sequence has 256 tokens and some has 64.
All inputs are finite; a program needn't handle non-finite values.
Results may differ from a plain program's by a relative error of at most 0.012.
Values may be sent and summed in bfloat16 or wider, within the bound.
A program may use at most 128 MiB of HBM per device.

v0:
```python
from functools import partial

import jax
import jax.numpy as jnp
from jax import lax
from jax.sharding import PartitionSpec as P

BLOCK = 64


epsilon = 1e-05


def to_blocks(value):
    return value.reshape((value.shape[0] // BLOCK, BLOCK) + value.shape[1:])


def silu_slope(values):
    sigma = jax.nn.sigmoid(values)
    return sigma * (1.0 + values * (1.0 - sigma))


def row_product(left, right):
    return lax.dot_general(
        left, right, (((0, 1), (0, 1)), ((), ())), preferred_element_type=jnp.float32
    )


def back_product(grad_rows, weight):
    return lax.dot_general(
        grad_rows, weight, (((2,), (1,)), ((), ())), preferred_element_type=jnp.float32
    )


def causal_conv(values, kernel_w):
    kernel = kernel_w.shape[0]
    length = values.shape[1]
    padded = jnp.pad(values, ((0, 0), (kernel - 1, 0), (0, 0)))
    return sum((kernel_w[offset] * padded[:, offset : offset + length] for offset in range(kernel)))


def forward_scan(step_size, active, b_rows, c_rows, decay_rate):

    def forward_position(current, row_data):
        dt_row, x_row, b_row, c_row = row_data
        current = (
            jnp.exp(dt_row[None, :] * decay_rate) * current
            + b_row[:, None] * (dt_row * x_row)[None, :]
        )
        return (current, jnp.sum(c_row[:, None] * current, axis=0))

    def advance(carried, pieces):
        final, outputs = lax.scan(forward_position, carried, pieces, unroll=8)
        return (final, (carried, outputs))

    zero_state = jnp.zeros(decay_rate.shape, jnp.float32)
    pieces = (to_blocks(step_size), to_blocks(active), to_blocks(b_rows), to_blocks(c_rows))
    unused, (starts, outputs) = lax.scan(advance, zero_state, pieces)
    return (starts, outputs.reshape(step_size.shape))


def backward_scan(starts, step_size, active, b_rows, c_rows, d_out, decay_rate):

    def remember(current, row_data):
        dt_row, x_row, b_row = row_data
        following = (
            jnp.exp(dt_row[None, :] * decay_rate) * current
            + b_row[:, None] * (dt_row * x_row)[None, :]
        )
        return (following, current)

    def backward_position(carry_pair, row_data):
        later, decay_sum = carry_pair
        prior, dt_row, x_row, b_row, c_row, d_row = row_data
        factor = jnp.exp(dt_row[None, :] * decay_rate)
        drive = dt_row * x_row
        state = factor * prior + b_row[:, None] * drive[None, :]
        adjoint = c_row[:, None] * d_row[None, :] + later
        weighted = adjoint * prior * factor
        lam_b = jnp.sum(adjoint * b_row[:, None], axis=0)
        d_step = x_row * lam_b + jnp.sum(weighted * decay_rate, axis=0)
        d_active = dt_row * lam_b
        d_b_row = jnp.sum(adjoint * drive[None, :], axis=1)
        d_c_row = jnp.sum(d_row[None, :] * state, axis=1)
        decay_sum = decay_sum + weighted * dt_row[None, :]
        return ((factor * adjoint, decay_sum), (d_active, d_step, d_b_row, d_c_row))

    def retreat(carry_pair, pieces):
        start_state, step_blk, active_blk, b_blk, c_blk, d_blk = pieces
        unused, priors = lax.scan(remember, start_state, (step_blk, active_blk, b_blk), unroll=8)
        return lax.scan(
            backward_position,
            carry_pair,
            (priors, step_blk, active_blk, b_blk, c_blk, d_blk),
            reverse=True,
            unroll=8,
        )

    zero_state = jnp.zeros(decay_rate.shape, jnp.float32)
    pieces = (
        starts,
        to_blocks(step_size),
        to_blocks(active),
        to_blocks(b_rows),
        to_blocks(c_rows),
        to_blocks(d_out),
    )
    (unused, decay_sum), (d_active, d_step, d_b_rows, d_c_rows) = lax.scan(
        retreat, (zero_state, zero_state), pieces, reverse=True
    )
    length = step_size.shape[0]
    return (
        d_active.reshape(length, -1),
        d_step.reshape(length, -1),
        d_b_rows.reshape(length, -1),
        d_c_rows.reshape(length, -1),
        decay_sum,
    )


def forward_pass(weights, tokens, lengths):
    gain, w_in, conv_w, conv_b, w_x, w_dt, dt_bias, a_log, d_skip, w_out = weights
    inner_width = w_out.shape[0]
    rank_width = w_dt.shape[0]
    state_width = a_log.shape[0]
    source = tokens.astype(jnp.float32)
    inv_rms = lax.rsqrt(jnp.mean(source * source, axis=-1, keepdims=True) + epsilon)
    normed = (source * inv_rms * gain.astype(jnp.float32)).astype(jnp.bfloat16)
    joined = jnp.dot(normed, w_in, preferred_element_type=jnp.float32)
    inner_part = joined[..., :inner_width]
    gate_part = joined[..., inner_width:]
    convolved = causal_conv(inner_part, conv_w.astype(jnp.float32)) + conv_b.astype(jnp.float32)
    active = jax.nn.silu(convolved).astype(jnp.bfloat16)
    active_wide = active.astype(jnp.float32)
    projected = jnp.dot(active, w_x, preferred_element_type=jnp.float32).astype(jnp.bfloat16)
    rank_part = projected[..., :rank_width]
    b_rows = projected[..., rank_width : rank_width + state_width].astype(jnp.float32)
    c_rows = projected[..., rank_width + state_width :].astype(jnp.float32)
    pre_step = jnp.dot(rank_part, w_dt, preferred_element_type=jnp.float32) + dt_bias.astype(
        jnp.float32
    )
    step_size = jax.nn.softplus(pre_step)
    decay_rate = -jnp.exp(a_log.astype(jnp.float32))
    starts, scan_out = jax.vmap(partial(forward_scan, decay_rate=decay_rate))(
        step_size, active_wide, b_rows, c_rows
    )
    mixed = scan_out + d_skip.astype(jnp.float32) * active_wide
    gate_act = jax.nn.silu(gate_part)
    gated = (mixed * gate_act).astype(jnp.bfloat16)
    branch = jnp.dot(gated, w_out, preferred_element_type=jnp.float32)
    positions = lax.broadcasted_iota(jnp.int32, tokens.shape[:2], 1)
    live = (positions < lengths[:, None]).astype(jnp.float32)[..., None]
    output = (source + live * branch).astype(jnp.bfloat16)
    saved = (
        source,
        inv_rms,
        normed,
        inner_part,
        gate_part,
        convolved,
        active,
        active_wide,
        rank_part,
        b_rows,
        c_rows,
        pre_step,
        step_size,
        starts,
        mixed,
        gate_act,
        gated,
        live,
    )
    return (output, saved)


def backward_pass(weights, saved, cotangent):
    gain, w_in, conv_w, conv_b, w_x, w_dt, dt_bias, a_log, d_skip, w_out = weights
    (
        source,
        inv_rms,
        normed,
        inner_part,
        gate_part,
        convolved,
        active,
        active_wide,
        rank_part,
        b_rows,
        c_rows,
        pre_step,
        step_size,
        starts,
        mixed,
        gate_act,
        gated,
        live,
    ) = saved
    decay_rate = -jnp.exp(a_log.astype(jnp.float32))
    cot_wide = cotangent.astype(jnp.float32)
    d_branch = (live * cot_wide).astype(jnp.bfloat16)
    grad_out = row_product(gated, d_branch)
    d_gated = back_product(d_branch, w_out)
    d_mixed = d_gated * gate_act
    d_gate = d_gated * mixed * silu_slope(gate_part)
    grad_skip = jnp.sum(d_mixed * active_wide, axis=(0, 1))
    d_active_scan, d_step, d_b_rows, d_c_rows, decay_sums = jax.vmap(
        partial(backward_scan, decay_rate=decay_rate)
    )(starts, step_size, active_wide, b_rows, c_rows, d_mixed)
    grad_a_log = jnp.sum(decay_sums, axis=0) * decay_rate
    d_pre = d_step * jax.nn.sigmoid(pre_step)
    grad_dt_bias = jnp.sum(d_pre, axis=(0, 1))
    d_pre_low = d_pre.astype(jnp.bfloat16)
    grad_dt = row_product(rank_part, d_pre_low)
    d_rank = back_product(d_pre_low, w_dt)
    d_projected = jnp.concatenate([d_rank, d_b_rows, d_c_rows], axis=-1).astype(jnp.bfloat16)
    grad_x = row_product(active, d_projected)
    d_active = d_mixed * d_skip.astype(jnp.float32) + d_active_scan + back_product(d_projected, w_x)
    d_conv = d_active * silu_slope(convolved)
    grad_conv_b = jnp.sum(d_conv, axis=(0, 1))
    kernel = conv_w.shape[0]
    length = source.shape[1]
    padded_in = jnp.pad(inner_part, ((0, 0), (kernel - 1, 0), (0, 0)))
    grad_conv_w = jnp.stack(
        [
            jnp.sum(d_conv * padded_in[:, offset : offset + length], axis=(0, 1))
            for offset in range(kernel)
        ]
    )
    padded_grad = jnp.pad(d_conv, ((0, 0), (0, kernel - 1), (0, 0)))
    conv_wide = conv_w.astype(jnp.float32)
    d_inner = sum(
        (
            conv_wide[offset] * padded_grad[:, kernel - 1 - offset : kernel - 1 - offset + length]
            for offset in range(kernel)
        )
    )
    d_joined = jnp.concatenate([d_inner, d_gate], axis=-1).astype(jnp.bfloat16)
    grad_in = row_product(normed, d_joined)
    d_normed = back_product(d_joined, w_in)
    grad_gain = jnp.sum(d_normed * source * inv_rms, axis=(0, 1))
    d_scaled = d_normed * gain.astype(jnp.float32)
    cubed = inv_rms * inv_rms * inv_rms
    d_source = inv_rms * d_scaled - source * cubed * jnp.mean(
        d_scaled * source, axis=-1, keepdims=True
    )
    input_grad = cot_wide + d_source
    return (
        input_grad,
        (
            grad_gain,
            grad_in,
            grad_conv_w,
            grad_conv_b,
            grad_x,
            grad_dt,
            grad_dt_bias,
            grad_a_log,
            grad_skip,
            grad_out,
        ),
    )


def body(
    tokens, lengths, cotangent, gain, w_in, conv_w, conv_b, w_x, w_dt, dt_bias, a_log, d_skip, w_out
):
    weights = (
        lax.all_gather(gain, "fsdp", axis=0, tiled=True),
        lax.all_gather(w_in, "fsdp", axis=0, tiled=True),
        lax.all_gather(conv_w, "fsdp", axis=1, tiled=True),
        lax.all_gather(conv_b, "fsdp", axis=0, tiled=True),
        lax.all_gather(w_x, "fsdp", axis=0, tiled=True),
        lax.all_gather(w_dt, "fsdp", axis=1, tiled=True),
        lax.all_gather(dt_bias, "fsdp", axis=0, tiled=True),
        lax.all_gather(a_log, "fsdp", axis=1, tiled=True),
        lax.all_gather(d_skip, "fsdp", axis=0, tiled=True),
        lax.all_gather(w_out, "fsdp", axis=0, tiled=True),
    )
    output, saved = forward_pass(weights, tokens, lengths)
    back_weights = (
        lax.all_gather(gain, "fsdp", axis=0, tiled=True),
        lax.all_gather(w_in, "fsdp", axis=0, tiled=True),
        lax.all_gather(conv_w, "fsdp", axis=1, tiled=True),
        lax.all_gather(conv_b, "fsdp", axis=0, tiled=True),
        lax.all_gather(w_x, "fsdp", axis=0, tiled=True),
        lax.all_gather(w_dt, "fsdp", axis=1, tiled=True),
        lax.all_gather(dt_bias, "fsdp", axis=0, tiled=True),
        lax.all_gather(a_log, "fsdp", axis=1, tiled=True),
        lax.all_gather(d_skip, "fsdp", axis=0, tiled=True),
        lax.all_gather(w_out, "fsdp", axis=0, tiled=True),
    )
    input_grad, grads = backward_pass(back_weights, saved, cotangent)
    (
        grad_gain,
        grad_in,
        grad_conv_w,
        grad_conv_b,
        grad_x,
        grad_dt,
        grad_dt_bias,
        grad_a_log,
        grad_skip,
        grad_out,
    ) = grads
    shards = (
        lax.psum_scatter(grad_gain, "fsdp", scatter_dimension=0, tiled=True),
        lax.psum_scatter(grad_in, "fsdp", scatter_dimension=0, tiled=True),
        lax.psum_scatter(grad_conv_w, "fsdp", scatter_dimension=1, tiled=True),
        lax.psum_scatter(grad_conv_b, "fsdp", scatter_dimension=0, tiled=True),
        lax.psum_scatter(grad_x, "fsdp", scatter_dimension=0, tiled=True),
        lax.psum_scatter(grad_dt, "fsdp", scatter_dimension=1, tiled=True),
        lax.psum_scatter(grad_dt_bias, "fsdp", scatter_dimension=0, tiled=True),
        lax.psum_scatter(grad_a_log, "fsdp", scatter_dimension=1, tiled=True),
        lax.psum_scatter(grad_skip, "fsdp", scatter_dimension=0, tiled=True),
        lax.psum_scatter(grad_out, "fsdp", scatter_dimension=0, tiled=True),
    )
    (
        part_gain,
        part_in,
        part_conv_w,
        part_conv_b,
        part_x,
        part_dt,
        part_dt_bias,
        part_a_log,
        part_skip,
        part_out,
    ) = shards
    owned = lax.psum(
        (
            part_gain,
            part_in,
            part_conv_w,
            part_conv_b,
            part_x,
            part_dt,
            part_dt_bias,
            part_a_log,
            part_skip,
            part_out,
        ),
        "dp",
    )
    (
        own_gain,
        own_in,
        own_conv_w,
        own_conv_b,
        own_x,
        own_dt,
        own_dt_bias,
        own_a_log,
        own_skip,
        own_out,
    ) = owned
    return (
        output,
        input_grad,
        own_gain,
        own_in,
        own_conv_w,
        own_conv_b,
        own_x,
        own_dt,
        own_dt_bias,
        own_a_log,
        own_skip,
        own_out,
    )


def solution(mesh):
    return jax.shard_map(
        body,
        mesh=mesh,
        in_specs=(
            P(("dp", "fsdp"), None, None),
            P(("dp", "fsdp")),
            P(("dp", "fsdp"), None, None),
            P("fsdp"),
            P("fsdp", None),
            P(None, "fsdp"),
            P("fsdp"),
            P("fsdp", None),
            P(None, "fsdp"),
            P("fsdp"),
            P(None, "fsdp"),
            P("fsdp"),
            P("fsdp", None),
        ),
        out_specs=(
            P(("dp", "fsdp"), None, None),
            P(("dp", "fsdp"), None, None),
            P("fsdp"),
            P("fsdp", None),
            P(None, "fsdp"),
            P("fsdp"),
            P("fsdp", None),
            P(None, "fsdp"),
            P("fsdp"),
            P(None, "fsdp"),
            P("fsdp"),
            P("fsdp", None),
        ),
        check_vma=False,
    )
```

profile of v0, /device:TPU:0, one launch (start us, length us, event | category | flops | bytes accessed | tf_op | source)
XLA Modules:
  0.0 944.2 jit_solution(8703928907951574462)
XLA Ops:
  32.6 8.2 all-gather.9.cloned.1.call-done
  40.8 6.6 multiply_reduce_fusion.32
  55.6 53.9 %while.139 = (s32[]{:T(128)}, f32[1,16,1536]{2,1,0:T(8,128)S(1)}, f32[4,1,16,1536]{3,2,1,0:T(8,128)}, f32[4,1,64,1536]{3,2,0,1:T(8,128)}, f32[4,1,64,1536]{3,0,2...) while((s32[]{:T(128)}, f32[1,16,1536]{2,1,0:T(8,128)S(1)}, ...), condition=%wide.region_12.13_spmd, body=%wide.region_1.12_spmd.sunk | while | flops 1769483 | bytes 4533250 | solution.py:58
  58.3 9.3 while.143
  71.8 9.3 while.143
  85.3 9.3 while.143
  98.8 9.3 while.143
  113.6 357.0 %while.142 = (s32[]{:T(128)}, f32[1,16,1536]{2,1,0:T(8,128)S(1)}, f32[1,16,1536]{2,1,0:T(8,128)S(1)}, f32[4,1,64,1536]{3,2,0,1:T(8,128)}, f32[4,1,64,1536]{3,2,0...) while((s32[]{:T(128)}, f32[1,16,1536]{2,1,0:T(8,128)S(1)}, ...), condition=%wide.region_50.51_spmd, body=%wide.region_13.50_spmd.sunk | while | flops 7065364 | bytes 16174039 | solution.py:108
  118.0 17.4 %while.144 = (s32[]{:T(128)}, f32[1,16,1536]{2,1,0:T(8,128)S(1)}, f32[8,8,1,16,1536]{4,3,1,2,0:T(8,128)}, f32[8,8,1,1536]{3,2,1,0:T(1,128)S(1)}, f32[16,1536]{1,...) while((s32[]{:T(128)}, f32[1,16,1536]{2,1,0:T(8,128)S(1)}, ...), condition=%wide.region_15.15_spmd, body=%wide.region_14.14_spmd.sunk | while | flops 1978377 | bytes 4892713 | solution.py:90
  137.3 63.9 %while.145 = (s32[]{:T(128)}, f32[1,16,1536]{2,1,0:T(8,128)S(1)}, f32[1,16,1536]{2,1,0:T(8,128)S(1)}, f32[8,8,1,1536]{3,2,1,0:T(1,128)S(1)}, f32[8,8,1,1536]{3,2...) while((s32[]{:T(128)}, f32[1,16,1536]{2,1,0:T(8,128)S(1)}, ...), condition=%wide.region_49.49_spmd, body=%wide.region_16.48_spmd.sunk | while | flops 5086984 | bytes 5521637 | solution.py:91
  207.2 17.4 %while.144 = (s32[]{:T(128)}, f32[1,16,1536]{2,1,0:T(8,128)S(1)}, f32[8,8,1,16,1536]{4,3,1,2,0:T(8,128)}, f32[8,8,1,1536]{3,2,1,0:T(1,128)S(1)}, f32[16,1536]{1,...) while((s32[]{:T(128)}, f32[1,16,1536]{2,1,0:T(8,128)S(1)}, ...), condition=%wide.region_15.15_spmd, body=%wide.region_14.14_spmd.sunk | while | flops 1978377 | bytes 4892713 | solution.py:90
  226.6 63.9 %while.145 = (s32[]{:T(128)}, f32[1,16,1536]{2,1,0:T(8,128)S(1)}, f32[1,16,1536]{2,1,0:T(8,128)S(1)}, f32[8,8,1,1536]{3,2,1,0:T(1,128)S(1)}, f32[8,8,1,1536]{3,2...) while((s32[]{:T(128)}, f32[1,16,1536]{2,1,0:T(8,128)S(1)}, ...), condition=%wide.region_49.49_spmd, body=%wide.region_16.48_spmd.sunk | while | flops 5086984 | bytes 5521637 | solution.py:91
  296.5 17.4 %while.144 = (s32[]{:T(128)}, f32[1,16,1536]{2,1,0:T(8,128)S(1)}, f32[8,8,1,16,1536]{4,3,1,2,0:T(8,128)}, f32[8,8,1,1536]{3,2,1,0:T(1,128)S(1)}, f32[16,1536]{1,...) while((s32[]{:T(128)}, f32[1,16,1536]{2,1,0:T(8,128)S(1)}, ...), condition=%wide.region_15.15_spmd, body=%wide.region_14.14_spmd.sunk | while | flops 1978377 | bytes 4892713 | solution.py:90
  315.8 63.9 %while.145 = (s32[]{:T(128)}, f32[1,16,1536]{2,1,0:T(8,128)S(1)}, f32[1,16,1536]{2,1,0:T(8,128)S(1)}, f32[8,8,1,1536]{3,2,1,0:T(1,128)S(1)}, f32[8,8,1,1536]{3,2...) while((s32[]{:T(128)}, f32[1,16,1536]{2,1,0:T(8,128)S(1)}, ...), condition=%wide.region_49.49_spmd, body=%wide.region_16.48_spmd.sunk | while | flops 5086984 | bytes 5521637 | solution.py:91
  385.7 17.4 %while.144 = (s32[]{:T(128)}, f32[1,16,1536]{2,1,0:T(8,128)S(1)}, f32[8,8,1,16,1536]{4,3,1,2,0:T(8,128)}, f32[8,8,1,1536]{3,2,1,0:T(1,128)S(1)}, f32[16,1536]{1,...) while((s32[]{:T(128)}, f32[1,16,1536]{2,1,0:T(8,128)S(1)}, ...), condition=%wide.region_15.15_spmd, body=%wide.region_14.14_spmd.sunk | while | flops 1978377 | bytes 4892713 | solution.py:90
  405.1 63.9 %while.145 = (s32[]{:T(128)}, f32[1,16,1536]{2,1,0:T(8,128)S(1)}, f32[1,16,1536]{2,1,0:T(8,128)S(1)}, f32[8,8,1,1536]{3,2,1,0:T(1,128)S(1)}, f32[8,8,1,1536]{3,2...) while((s32[]{:T(128)}, f32[1,16,1536]{2,1,0:T(8,128)S(1)}, ...), condition=%wide.region_49.49_spmd, body=%wide.region_16.48_spmd.sunk | while | flops 5086984 | bytes 5521637 | solution.py:91
  492.4 5.1 fusion.176
  500.1 4.7 fusion.187
  516.6 11.3 %reduce-scatter.11.cloned.1.call-done = f32[768,80]{0,1:T(8,128)} async-done(((f32[1536,80]{0,1:T(8,128)}), f32[768,80]{0,1:T(8,128)}) %reduce-scatter.11.cloned.1.call-update) | async-done | bytes 245776 | tf_op jit(solution)/shard_map/reduce_scatter | solution.py:311
  527.9 16.8 %reduce-scatter.17.cloned.1.call-done = f32[768,768]{1,0:T(8,128)} async-done(((f32[1536,768]{1,0:T(8,128)}), f32[768,768]{1,0:T(8,128)}) %reduce-scatter.17.cloned.1.call-update) | async-done | bytes 2359312 | tf_op jit(solution)/shard_map/reduce_scatter | solution.py:316
  544.7 21.3 %reduce-scatter.9.cloned.1.call-done = f32[384,3072]{1,0:T(8,128)} async-done(((f32[768,3072]{1,0:T(8,128)}), f32[384,3072]{1,0:T(8,128)}) %reduce-scatter.9.cloned.1.call-update) | async-done | bytes 4718608 | tf_op jit(solution)/shard_map/reduce_scatter | solution.py:308
  569.9 111.1 %all-reduce.12.cloned.1.call-done = (f32[384]{0:T(512)}, f32[4,768]{1,0:T(4,128)}, f32[768]{0:T(1024)}, f32[768]{0:T(1024)}, f32[16,768]{1,0:T(8,128)}, /*index=5*/f32[768]{0:T(1024)}) async-done(((f32[384]{0:T(512)}, f32[4,768]{1,0:T(4,128)}, f32[768]{0:T(1024)}, f32[768]{0:T(1024)}, f32[16,768]{1,0:T(8,128)}, /*index=5*/f32[768]{0:T(1024)}), (f32[384]{0:T(512)}, f32[4,768]{1,0:T(4,128)}, f32[768]{0:T(1024)}, ...) | async-done | bytes 72208 | tf_op jit(solution)/shard_map/psum | solution.py:330
  681.0 244.1 %all-reduce.14.cloned.1.call-done = (f32[384,3072]{1,0:T(8,128)}, f32[768,80]{0,1:T(8,128)}, f32[48,768]{1,0:T(8,128)}, f32[768,768]{1,0:T(8,128)}) async-done(((f32[384,3072]{1,0:T(8,128)}, f32[768,80]{0,1:T(8,128)}, f32[48,768]{1,0:T(8,128)}, f32[768,768]{1,0:T(8,128)}), (f32[384,3072]{1,0:T(8,128)}, f32[768,80]{0,1:T(8,128)}, f32[48,768]{1,0:T(8,128)}, ...) | async-done | bytes 7471120 | tf_op jit(solution)/shard_map/psum | solution.py:330
  926.4 5.2 copy.244
  (3124 shorter events, 477.2 us)
Async XLA Ops:
  7.2 9.8 %copy-start.53 = (bf16[768]{0:T(1024)(128)(2,1)S(1)}, bf16[768]{0:T(1024)(128)(2,1)}, u32[]{:S(2)}) copy-start(bf16[768]{0:T(1024)(128)(2,1)} %param.34) | copy-start | bytes 4612
  7.2 12.2 %copy-start.43 = (bf16[16,768]{1,0:T(8,128)(2,1)S(1)}, bf16[16,768]{1,0:T(8,128)(2,1)}, u32[]{:S(2)}) copy-start(bf16[16,768]{1,0:T(8,128)(2,1)} %param.33) | copy-start | bytes 73732
  7.2 14.0 %copy-start.30 = (bf16[48,768]{1,0:T(8,128)(2,1)S(1)}, bf16[48,768]{1,0:T(8,128)(2,1)}, u32[]{:S(2)}) copy-start(bf16[48,768]{1,0:T(8,128)(2,1)} %param.31) | copy-start | bytes 221188
  7.3 15.9 %copy-start.26 = (bf16[768,80]{0,1:T(8,128)(2,1)S(1)}, bf16[768,80]{0,1:T(8,128)(2,1)}, u32[]{:S(2)}) copy-start(bf16[768,80]{0,1:T(8,128)(2,1)} %param.30) | copy-start | bytes 368644
  7.3 19.7 %all-gather.7.cloned.1.call-start = ((), (), s32[]{:S(2)}) async-start(), calls=%async_computation.6 | async-start | bytes 7077888 | tf_op jit(solution)/shard_map/all_gather | solution.py:270
  8.0 17.4 %copy-start.6 = (bf16[1,256,768]{2,1,0:T(8,128)(2,1)S(1)}, bf16[1,256,768]{2,1,0:T(8,128)(2,1)}, u32[]{:S(2)}) copy-start(bf16[1,256,768]{2,1,0:T(8,128)(2,1)} %param.23) | copy-start | bytes 1179652
  8.0 32.8 %all-gather.9.cloned.1.call-start = ((), (), s32[]{:S(2)}) async-start(), calls=%async_computation.7 | async-start | bytes 3538944 | tf_op jit(solution)/shard_map/all_gather | solution.py:278
  8.8 502.1 %reduce-scatter.19.cloned.1.call-start = ((), (), s32[]{:S(2)}) async-start(), calls=%async_computation.13 | async-start | bytes 1179648
  10.8 20.0 %copy-start.20 = (f32[768]{0:T(1024)}, f32[768]{0:T(1024)S(1)}, u32[]{:S(2)}) copy-start(f32[768]{0:T(1024)S(1)} %reshape.5254) | copy-start | bytes 9220
  25.3 22.1 %copy-start.13 = (bf16[1536,80]{0,1:T(8,128)(2,1)}, bf16[1536,80]{0,1:T(8,128)(2,1)S(1)}, u32[]{:S(2)}) copy-start(bf16[1536,80]{0,1:T(8,128)(2,1)S(1)} %all_gather.42) | copy-start | bytes 737284
  25.3 15.5 %copy-start.55 = (f32[256]{0:T(256)}, f32[256]{0:T(256)S(1)}, u32[]{:S(2)}) copy-start(f32[256]{0:T(256)S(1)} %compare_convert_fusion) | copy-start | bytes 3076
  25.4 15.4 %copy-start.32 = (f32[1536]{0:T(1024)}, f32[1536]{0:T(1024)S(1)}, u32[]{:S(2)}) copy-start(f32[1536]{0:T(1024)S(1)} %get-tuple-element.940) | copy-start | bytes 18436
  25.4 15.4 %copy-start.34 = (f32[1536]{0:T(1024)}, f32[1536]{0:T(1024)S(1)}, u32[]{:S(2)}) copy-start(f32[1536]{0:T(1024)S(1)} %get-tuple-element.941) | copy-start | bytes 18436
  25.4 15.4 %copy-start.36 = (f32[1536]{0:T(1024)}, f32[1536]{0:T(1024)S(1)}, u32[]{:S(2)}) copy-start(f32[1536]{0:T(1024)S(1)} %get-tuple-element.942) | copy-start | bytes 18436
  25.5 15.4 %copy-start.38 = (f32[1536]{0:T(1024)}, f32[1536]{0:T(1024)S(1)}, u32[]{:S(2)}) copy-start(f32[1536]{0:T(1024)S(1)} %get-tuple-element.943) | copy-start | bytes 18436
  32.6 14.8 %copy-start.3 = (f32[1,256,1536]{2,1,0:T(8,128)}, f32[1,256,1536]{2,1,0:T(8,128)S(1)}, u32[]{:S(2)}) copy-start(f32[1,256,1536]{2,1,0:T(8,128)S(1)} %slice.679) | copy-start | bytes 4718596
  484.0 28.6 %reduce-scatter.15.cloned.1.call-start = ((), (), s32[]{:S(2)}) async-start(), calls=%async_computation.11 | async-start | bytes 147456 | tf_op jit(solution)/shard_map/reduce_scatter | solution.py:314
  484.8 31.8 %reduce-scatter.13.cloned.1.call-start = ((), (), s32[]{:S(2)}) async-start(), calls=%async_computation.10 | async-start | bytes 442368 | tf_op jit(solution)/shard_map/reduce_scatter | solution.py:312
  485.8 42.1 %reduce-scatter.11.cloned.1.call-start = ((), (), s32[]{:S(2)}) async-start(), calls=%async_computation.9 | async-start | bytes 737280 | tf_op jit(solution)/shard_map/reduce_scatter | solution.py:311
  487.0 57.7 %reduce-scatter.17.cloned.1.call-start = ((), (), s32[]{:S(2)}) async-start(), calls=%async_computation.12 | async-start | bytes 7077888 | tf_op jit(solution)/shard_map/reduce_scatter | solution.py:316
  491.1 74.8 %reduce-scatter.9.cloned.1.call-start = ((), (), s32[]{:S(2)}) async-start(), calls=%async_computation.8 | async-start | bytes 14155776 | tf_op jit(solution)/shard_map/reduce_scatter | solution.py:308
  497.5 183.4 %all-reduce.12.cloned.1.call-start = ((), (), s32[]{:S(2)}) async-start(), calls=%async_computation.14 | async-start | bytes 151552 | tf_op jit(solution)/shard_map/psum | solution.py:330
  512.6 412.4 %all-reduce.14.cloned.1.call-start = ((), (), s32[]{:S(2)}) async-start(), calls=%async_computation.15 | async-start | bytes 14942208 | tf_op jit(solution)/shard_map/psum | solution.py:330
  926.4 9.6 %copy-start.9 = (f32[768,768]{1,0:T(8,128)S(1)}, f32[768,768]{1,0:T(8,128)}, u32[]{:S(2)}) copy-start(f32[768,768]{1,0:T(8,128)} %get-tuple-element.2276) | copy-start | bytes 7077892
  (46 other events, 168.5 us)
Sparse Core Ops, SparseCore 0:
  9.6 17.3 all-gather.6
  28.5 12.2 all-gather.8
  484.1 9.4 reduce-scatter.18
  496.3 8.6 reduce-scatter.14
  507.7 8.8 reduce-scatter.12
  518.8 9.0 reduce-scatter.10
  530.9 13.7 reduce-scatter.16
  547.0 18.9 reduce-scatter.8
  573.5 107.3 all-reduce.11
  687.2 237.7 all-reduce.13
where the time goes:
time: 951 us; the launch traced here: 944 us
  waiting for transfers between devices  419 us (44%)
  other arithmetic  283 us (30%)
  local copies, waits for them, and re-layouts  160 us (17%)
  matrix products  31.5 us (3%)
  blocking collectives  18.4 us (2%)
  between operations  16.8 us (2%)
  loops' own time  15.9 us (2%)
    psum x2, waiting for transfers between devices, body(): lax.psum((part_gain, part_in, part_conv_w, part_conv_b, part_x, part_dt,...  355 us
    reduce_sum x96, other arithmetic, backward_position(): d_step = x_row * lam_b + jnp.sum(weighted * decay_rate, axis=0)  127 us
    add x32, other arithmetic, backward_position(): decay_sum = decay_sum + weighted * dt_row[None, :]  48.2 us
    reduce_sum x32, other arithmetic, backward_position(): d_c_row = jnp.sum(d_row[None, :] * state, axis=1)  42.3 us
    dynamic_slice x32, local copies, waits for them, and re-layouts, forward_scan(): unused, (starts, outputs) = lax.scan(advance, zero_state, pieces)  30.7 us
    dynamic_update_slice x32, local copies, waits for them, and re-layouts, retreat(): lax.scan(remember, start_state, (step_blk, active_blk, b_blk), unroll=8)  30.6 us
    unnamed x141, local copies, waits for them, and re-layouts  26 us
    while x416, other arithmetic  24.2 us
  transfers between devices with their start and end apart: 10, of which 8 were waited for; matrix products, arithmetic and copies ran while one was open for 3% of the time, Pallas kernels for 0%

commit v1 on v0

v1 whole, which is shorter than its diff:
```python
import functools
import jax
import jax.numpy as jnp
from jax import lax
from jax.experimental import pallas as pl
from jax.experimental.pallas import tpu as pltpu
from jax.sharding import PartitionSpec as P

F32 = jnp.float32
BF16 = jnp.bfloat16
EPS = 1e-05
STEPS = 16
LOG2E = 1.4426950408889634
VMEM = pl.BlockSpec(memory_space=pltpu.VMEM)
SMEM = pl.BlockSpec(memory_space=pltpu.SMEM)
MB = 2**20


def dot(left, right, over=(1, 0)):
    dims = (((over[0],), (over[1],)), ((), ()))
    return lax.dot_general(left, right, dims, preferred_element_type=F32)


def each(count, width, step):
    def run(index, carry):
        step(pl.ds(pl.multiple_of(index * width, width), width))
        return carry

    lax.fori_loop(0, count, run, 0)


def rows_of(block, size):
    return pl.ds(pl.multiple_of(block * size, size), size)


def compute_kernel(
    length_ref, tok, cot, gain, w_in, conv_w, conv_b, w_x, w_dt, dt_bias, a_log, d_skip, w_out,
    output, input_grad, normed, gated, d_branch, d_joined, g_gain, g_rows, g_dt, g_xt,
    inv, inner, gact, gslope, cslope, active, proj, cmat, bmat, spread, decay,
    step_s, drive, sigp, mixed, d_mixed, lam_b, d_decay, states, carry, lam_s, part_s,
    db, dc, d_pre_low, d_proj, d_conv, d_normed,
):
    T, D = tok.shape
    E = w_out.shape[0]
    N = a_log.shape[0]
    R = w_dt.shape[0]
    J = w_x.shape[1]
    K = conv_w.shape[0]
    NB = T // STEPS
    WIDE = STEPS * N
    PAD = 8

    def prepare(block, c):
        rows = rows_of(block, 64)
        x = tok[rows, :].astype(F32)
        scale = lax.rsqrt(jnp.mean(x * x, axis=1, keepdims=True) + EPS)
        inv[rows, :] = jnp.broadcast_to(scale, (64, 128))
        normed[rows, :] = (x * scale * gain[...].astype(F32)).astype(BF16)
        at = block * 64 + lax.broadcasted_iota(jnp.int32, (64, 1), 0)
        live = (at < length_ref[0]).astype(F32)
        d_branch[rows, :] = (live * cot[rows, :].astype(F32)).astype(BF16)
        return c

    lax.fori_loop(0, T // 64, prepare, 0)

    inner[pl.ds(0, PAD), :] = jnp.zeros((PAD, E), F32)

    def project_in(cols):
        inner[pl.ds(PAD, T), cols] = dot(normed[...], w_in[:, cols])

    each(E // 256, 256, project_in)

    def convolve(cols):
        taps = conv_w[:, cols].astype(F32)
        value = conv_b[:, cols].astype(F32) + sum(
            taps[k : k + 1] * inner[pl.ds(PAD - K + 1 + k, T), cols] for k in range(K)
        )
        sigma = jax.nn.sigmoid(value)
        active[:, cols] = (value * sigma).astype(BF16)
        cslope[:, cols] = sigma * (1.0 + value * (1.0 - sigma))

    each(E // 128, 128, convolve)

    def project_gate(index, c):
        source = pl.ds(pl.multiple_of(E + index * 256, 256), 256)
        cols = rows_of(index, 256)
        value = dot(normed[...], w_in[:, source])
        sigma = jax.nn.sigmoid(value)
        gact[:, cols] = value * sigma
        gslope[:, cols] = sigma * (1.0 + value * (1.0 - sigma))
        return c

    lax.fori_loop(0, E // 256, project_gate, 0)

    proj[...] = dot(active[...], w_x[...]).astype(BF16)

    row = lax.broadcasted_iota(jnp.int32, (J, WIDE), 0)
    col = lax.broadcasted_iota(jnp.int32, (J, WIDE), 1)
    at = lax.broadcasted_iota(jnp.int32, (T, WIDE), 0)
    to = lax.broadcasted_iota(jnp.int32, (T, WIDE), 1)
    diagonal = (at % STEPS == to // N).astype(F32)
    pick_b = (row == R + col % N).astype(BF16)
    pick_c = (row == R + N + col % N).astype(BF16)
    bmat[...] = (dot(proj[...], pick_b) * diagonal).astype(BF16)
    cmat[...] = (dot(proj[...], pick_c) * diagonal).astype(BF16)
    ones = jnp.ones((STEPS, 128), BF16)

    def spread_rows(source):
        def run(block, c):
            spread[rows_of(block, WIDE), :] = dot(source[rows_of(block, STEPS), :], ones, (0, 0))
            return c

        lax.fori_loop(0, NB, run, 0)

    spread_rows(bmat)

    def step_size(cols):
        pre = dot(proj[:, :R], w_dt[:, cols]) + dt_bias[:, cols].astype(F32)
        size = jnp.maximum(pre, 0.0) + jnp.log1p(jnp.exp(-jnp.abs(pre)))
        step_s[:, cols] = size
        sigp[:, cols] = jax.nn.sigmoid(pre)
        drive[:, cols] = size * active[:, cols].astype(F32)

    each(E // 256, 256, step_size)
    decay[...] = -jnp.exp(a_log[...].astype(F32)) * LOG2E

    states[pl.ds(0, N), :] = jnp.zeros((N, E), BF16)

    def scan_sum(block):
        rows = rows_of(block, STEPS)
        held = states[pl.ds(pl.multiple_of(block * WIDE + N, N), WIDE), :]
        mixed[rows, :] = dot(cmat[rows, :], held)

    def forward_block(block, state):
        scan_sum(jnp.maximum(block - 1, 0))
        rows = rows_of(block, STEPS)
        size, push = step_s[rows, :], drive[rows, :]
        for i in range(STEPS):
            t = block * STEPS + i
            b_row = spread[rows_of(t, N), :]
            b_row = jnp.concatenate([b_row] * (E // 128), axis=1)
            factor = jnp.exp2(jnp.broadcast_to(size[i : i + 1], (N, E)) * decay[...])
            state = factor * state + b_row * jnp.broadcast_to(push[i : i + 1], (N, E))
            states[rows_of(t + 1, N), :] = state.astype(BF16)
        return state

    lax.fori_loop(0, NB, forward_block, jnp.zeros((N, E), F32))
    scan_sum(NB - 1)

    def mix(cols):
        value = mixed[:, cols] + d_skip[:, cols].astype(F32) * active[:, cols].astype(F32)
        mixed[:, cols] = value
        gated[:, cols] = (value * gact[:, cols]).astype(BF16)

    each(E // 128, 128, mix)

    def project_out(cols):
        branch = dot(gated[...], w_out[:, cols])
        at = lax.broadcasted_iota(jnp.int32, (T, 1), 0)
        live = (at < length_ref[0]).astype(F32)
        output[:, cols] = (tok[:, cols].astype(F32) + live * branch).astype(BF16)

    each(D // 256, 256, project_out)

    def back_out(index, c):
        cols = rows_of(index, 256)
        d_gated = dot(d_branch[...], w_out[cols, :], (1, 1))
        d_value = d_gated * gact[:, cols]
        d_mixed[:, cols] = d_value
        to = pl.ds(pl.multiple_of(E + index * 256, 256), 256)
        d_joined[:, to] = (d_gated * mixed[:, cols] * gslope[:, cols]).astype(BF16)
        g_rows[pl.ds(N + K + 2, 1), cols] = jnp.sum(
            d_value * active[:, cols].astype(F32), axis=0, keepdims=True
        )
        return c

    lax.fori_loop(0, E // 256, back_out, 0)

    spread_rows(cmat)
    carry[...] = jnp.zeros((N, E), F32)
    g_rows[pl.ds(0, N), :] = jnp.zeros((N, E), F32)
    half = N // 2
    at = lax.broadcasted_iota(jnp.int32, (STEPS, STEPS * half), 0)
    to = lax.broadcasted_iota(jnp.int32, (STEPS, STEPS * half), 1)
    gather = (at == to // half).astype(BF16)
    CH = 256

    def backward_block(k, c):
        block = NB - 1 - k
        rows = rows_of(block, STEPS)
        for chunk in range(E // CH):
            cols = pl.ds(chunk * CH, CH)
            later, total = carry[:, cols], g_rows[pl.ds(0, N), cols]
            size, d_value = step_s[rows, cols], d_mixed[rows, cols]
            rate = decay[:, cols]
            for i in reversed(range(STEPS)):
                t = block * STEPS + i
                dt = jnp.broadcast_to(size[i : i + 1], (N, CH))
                c_row = spread[rows_of(t, N), :]
                c_row = jnp.concatenate([c_row] * (CH // 128), axis=1)
                lam = c_row * jnp.broadcast_to(d_value[i : i + 1], (N, CH)) + later
                lam_s[pl.ds(i * N, N), cols] = lam.astype(BF16)
                later = jnp.exp2(dt * rate) * lam
                weighted = later * states[rows_of(t, N), cols].astype(F32)
                total = total + weighted * dt
                part = weighted * rate
                part = part[:half] + part[half:]
                if i % 2 == 1:
                    odd = part
                else:
                    part_s[pl.ds(i * half, N), cols] = jnp.concatenate([part, odd], axis=0).astype(BF16)
            carry[:, cols] = later
            g_rows[pl.ds(0, N), cols] = total
            held = lam_s[:, cols]
            lam_b[rows, cols] = dot(bmat[rows, :], held)
            d_decay[rows, cols] = dot(gather, part_s[:, cols])
            b_part = dot(drive[rows, cols].astype(BF16), held, (1, 1))
            after = states[pl.ds(pl.multiple_of(block * WIDE + N, N), WIDE), cols]
            c_part = dot(d_value.astype(BF16), after, (1, 1))
            if chunk == 0:
                db[rows, :] = b_part
                dc[rows, :] = c_part
            else:
                db[rows, :] += b_part
                dc[rows, :] += c_part
        return c

    lax.fori_loop(0, NB, backward_block, 0)
    g_rows[pl.ds(0, N), :] = g_rows[pl.ds(0, N), :] * decay[...] * (1.0 / LOG2E)

    def back_step(cols):
        wide = active[:, cols].astype(F32)
        adjoint = lam_b[:, cols]
        d_pre = (wide * adjoint + d_decay[:, cols] * (1.0 / LOG2E)) * sigp[:, cols]
        g_rows[pl.ds(N + K + 1, 1), cols] = jnp.sum(d_pre, axis=0, keepdims=True)
        d_pre_low[:, cols] = d_pre.astype(BF16)
        d_mixed[:, cols] = d_mixed[:, cols] * d_skip[:, cols].astype(F32) + step_s[:, cols] * adjoint

    each(E // 128, 128, back_step)

    row = lax.broadcasted_iota(jnp.int32, (WIDE, N), 0)
    col = lax.broadcasted_iota(jnp.int32, (WIDE, N), 1)
    pick = (row % N == col).astype(BF16)
    d_proj[:, pl.ds(0, R)] = dot(d_pre_low[...], w_dt[...], (1, 1)).astype(BF16)
    d_proj[:, pl.ds(R, N)] = dot((db[...] * diagonal).astype(BF16), pick).astype(BF16)
    d_proj[:, pl.ds(R + N, N)] = dot((dc[...] * diagonal).astype(BF16), pick).astype(BF16)

    d_conv[pl.ds(T, PAD), :] = jnp.zeros((PAD, E), F32)

    def back_conv(cols):
        g_dt[:, cols] = dot(proj[:, :R], d_pre_low[:, cols], (0, 0))
        g_xt[:, cols] = dot(d_proj[...], active[:, cols], (0, 0))
        d_active = d_mixed[:, cols] + dot(d_proj[...], w_x[cols, :], (1, 1))
        d_value = d_active * cslope[:, cols]
        d_conv[pl.ds(0, T), cols] = d_value
        g_rows[pl.ds(N + K, 1), cols] = jnp.sum(d_value, axis=0, keepdims=True)
        taps = conv_w[:, cols].astype(F32)
        total = jnp.zeros_like(d_value)
        for k in range(K):
            g_rows[pl.ds(N + k, 1), cols] = jnp.sum(
                d_value * inner[pl.ds(PAD - K + 1 + k, T), cols], axis=0, keepdims=True
            )
            total = total + taps[k : k + 1] * d_conv[pl.ds(K - 1 - k, T), cols]
        d_joined[:, cols] = total.astype(BF16)

    each(E // 128, 128, back_conv)
    g_rows[pl.ds(N + K + 3, 1), :] = jnp.zeros((1, E), F32)

    def back_in(index, c):
        rows = rows_of(index, 256)
        d_normed[:, rows] = dot(d_joined[...], w_in[rows, :], (1, 1))
        return c

    lax.fori_loop(0, D // 256, back_in, 0)

    g_gain[...] = jnp.zeros((1, D), F32)

    def back_norm(block, c):
        rows = rows_of(block, 64)
        x = tok[rows, :].astype(F32)
        scale = inv[rows, pl.ds(0, 1)]
        d_value = d_normed[rows, :]
        g_gain[...] += jnp.sum(d_value * x * scale, axis=0, keepdims=True)
        d_scaled = d_value * gain[...].astype(F32)
        shared = jnp.mean(d_scaled * x, axis=1, keepdims=True)
        input_grad[rows, :] = (
            cot[rows, :].astype(F32) + scale * d_scaled - x * (scale * scale * scale) * shared
        )
        return c

    lax.fori_loop(0, T // 64, back_norm, 0)


def compute(length, tokens, cotangent, gain, w_in, conv_w, conv_b, w_x, w_dt, dt_bias, a_log, d_skip, w_out):
    T, D = tokens.shape
    E, N, R, J, K = w_out.shape[0], a_log.shape[0], w_dt.shape[0], w_x.shape[1], conv_w.shape[0]
    wide = STEPS * N
    full = pltpu.VMEM((T, E), F32)
    low = pltpu.VMEM((T, E), BF16)
    out = lambda shape, dtype=F32: jax.ShapeDtypeStruct(shape, dtype)
    return pl.pallas_call(
        compute_kernel,
        out_shape=[
            out((T, D), BF16), out((T, D)), out((T, D), BF16), out((T, E), BF16), out((T, D), BF16),
            out((T, 2 * E), BF16), out((1, D)), out((N + K + 4, E)), out((R, E)), out((J, E)),
        ],
        in_specs=[SMEM] + [VMEM] * 12,
        out_specs=[VMEM] * 10,
        scratch_shapes=[
            pltpu.VMEM((T, 128), F32), pltpu.VMEM((T + 8, E), F32), full, full, full, low,
            pltpu.VMEM((T, J), BF16), pltpu.VMEM((T, wide), BF16), pltpu.VMEM((T, wide), BF16),
            pltpu.VMEM((T * N, 128), F32), pltpu.VMEM((N, E), F32),
            full, full, full, full, full, full, full, pltpu.VMEM(((T + 1) * N, E), BF16),
            pltpu.VMEM((N, E), F32), pltpu.VMEM((wide, E), BF16), pltpu.VMEM((wide // 2, E), BF16),
            pltpu.VMEM((T, wide), F32), pltpu.VMEM((T, wide), F32), low, pltpu.VMEM((T, J), BF16),
            pltpu.VMEM((T + 8, E), F32), pltpu.VMEM((T, D), F32),
        ],
        compiler_params=pltpu.CompilerParams(vmem_limit_bytes=62 * MB),
        name="layer",
    )(length, tokens, cotangent, gain, w_in, conv_w, conv_b, w_x, w_dt, dt_bias, a_log, d_skip, w_out)


def gather(weights):
    axes = (0, 0, 1, 0, 0, 1, 0, 1, 0, 0)
    return [lax.all_gather(w, "fsdp", axis=a, tiled=True) for w, a in zip(weights, axes)]


def reduce_plain(normed, gated, d_branch, d_joined, g_gain, g_rows, g_dt, g_xt):
    N, K = g_rows.shape[0] - 8, 4
    big_in = lax.dot_general(normed, d_joined, (((0,), (0,)), ((), ())), preferred_element_type=F32)
    big_out = lax.dot_general(gated, d_branch, (((0,), (0,)), ((), ())), preferred_element_type=F32)
    rows = jnp.concatenate([g_rows, g_dt, g_xt], axis=0)

    def scatter(value, axis):
        return lax.psum_scatter(value, "fsdp", scatter_dimension=axis, tiled=True)

    own = (
        scatter(big_in.astype(BF16), 0), scatter(big_out.astype(BF16), 0),
        scatter(rows, 1), scatter(g_gain[0], 0),
    )
    own_in, own_out, own_rows, own_gain = lax.psum(own, "dp")
    return own_in.astype(F32), own_out.astype(F32), own_rows, own_gain


def body(
    tokens, lengths, cotangent, gain, w_in, conv_w, conv_b, w_x, w_dt, dt_bias, a_log, d_skip, w_out
):
    weights = gather((gain, w_in, conv_w, conv_b, w_x, w_dt, dt_bias, a_log, d_skip, w_out))
    weights = [w.reshape(1, -1) if w.ndim == 1 else w for w in weights]
    output, input_grad, *parts = compute(lengths, tokens[0], cotangent[0], *weights)
    own_in, own_out, rows, own_gain = reduce_plain(*parts)
    N, K, R = a_log.shape[0], conv_w.shape[0], w_dt.shape[0]
    M = N + K + 4
    return (
        output[None], input_grad[None], own_gain, own_in, rows[N : N + K], rows[N + K],
        rows[M + R :].T, rows[M : M + R], rows[N + K + 1], rows[:N], rows[N + K + 2], own_out,
    )


def solution(mesh):
    seq, row, col, one = P(("dp", "fsdp"), None, None), P("fsdp", None), P(None, "fsdp"), P("fsdp")
    return jax.shard_map(
        body,
        mesh=mesh,
        in_specs=(seq, P(("dp", "fsdp")), seq, one, row, col, one, row, col, one, col, one, row),
        out_specs=(seq, seq, one, row, col, one, row, col, one, col, one, row),
        check_vma=False,
    )
```

time: 951 us -> 424 us (0.45)
  other arithmetic: 283 us -> 8.34 us
  local copies, waits for them, and re-layouts: 160 us -> 8.39 us
  waiting for transfers between devices: 419 us -> 272 us
  Pallas kernels: 0 us -> 52.1 us
  blocking collectives: 18.4 us -> 60.9 us
  matrix products: 31.5 us -> 5.85 us
  loops' own time: 15.9 us -> 0 us
    reduce_sum x227 -> x0, other arithmetic: 194 us -> none  [the longest x96 127 us: backward_position(): d_step = x_row * lam_b + jnp.sum(weighted * decay_rate, axis=0)]
    psum x2, waiting for transfers between devices: 355 us -> 221 us  [reduce_plain(): own_in, own_out, own_rows, own_gain = lax.psum(own, 'dp')]
    add x66 -> x0, other arithmetic: 54.7 us -> none  [the longest x32 48.2 us: backward_position(): decay_sum = decay_sum + weighted * dt_row[None, :]]
    pallas_call x0 -> x1, Pallas kernels: none -> 52.1 us  [compute(): pl.pallas_call(compute_kernel, out_shape=[out((T, D), BF16), out((T, D)),...]
    dynamic_update_slice x144 -> x0, local copies, waits for them, and re-layouts: 44.5 us -> none  [the longest x32 30.6 us: retreat(): lax.scan(remember, start_state, (step_blk, active_blk, b_blk), unroll=8)]
    psum x0 -> x1, blocking collectives: none -> 42.5 us  [reduce_plain(): own_in, own_out, own_rows, own_gain = lax.psum(own, 'dp')]
    dynamic_slice x32 -> x0, local copies, waits for them, and re-layouts: 30.7 us -> none  [forward_scan(): unused, (starts, outputs) = lax.scan(advance, zero_state, pieces)]
    dot_general x12 -> x2, matrix products: 31.5 us -> 5.85 us  [the longest x1 3.61 us: reduce_plain(): lax.dot_general(normed, d_joined, (((0,), (0,)), ((), ())), preferred_ele...]
  transfers between devices with their start and end apart: 10 -> 7, of which waited for: 8 -> 6; matrix products, arithmetic and copies ran while one was open for 3% -> 3% of each run, Pallas kernels for 0% -> 0%
where the time goes in v1:
time: 424 us; the launch traced here: 423 us
  waiting for transfers between devices  272 us (64%)
  blocking collectives  60.9 us (14%)
  Pallas kernels  52.1 us (12%)
  between operations  15.7 us (4%)
  local copies, waits for them, and re-layouts  8.39 us (2%)
  other arithmetic  8.34 us (2%)
  matrix products  5.85 us (1%)
    psum x2, waiting for transfers between devices, reduce_plain(): own_in, own_out, own_rows, own_gain = lax.psum(own, 'dp')  221 us
    pallas_call x1, Pallas kernels, compute(): pl.pallas_call(compute_kernel, out_shape=[out((T, D), BF16), out((T, D)),...  52.1 us
    psum x1, blocking collectives, reduce_plain(): own_in, own_out, own_rows, own_gain = lax.psum(own, 'dp')  42.5 us
    reduce_scatter x3, waiting for transfers between devices, scatter(): return lax.psum_scatter(value, 'fsdp', scatter_dimension=axis, tiled=True)  34 us
    all_gather x8, blocking collectives, gather(): lax.all_gather(w, 'fsdp', axis=a, tiled=True)  15.9 us
    all_gather x2, waiting for transfers between devices, gather(): lax.all_gather(w, 'fsdp', axis=a, tiled=True)  14.9 us
  transfers between devices with their start and end apart: 7, of which 6 were waited for; matrix products, arithmetic and copies ran while one was open for 3% of the time, Pallas kernels for 0%

profile of v1, /device:TPU:0, one launch (start us, length us, event | category | flops | bytes accessed | tf_op | source)
XLA Modules:
  0.0 423.3 jit_solution(10741487539344623148)
XLA Ops:
  9.7 1.9 all-gather
  11.6 1.9 all-gather.1
  13.5 1.9 all-gather.2
  15.4 1.9 all-gather.3
  17.4 1.9 all_gather.32.conv_w
  19.3 2.0 all_gather.37.a_log
  21.3 2.1 all_gather.35.w_dt
  23.4 2.2 all_gather.34.w_x
  25.6 14.9 %all-gather.7.cloned.1.call-done.w_in = bf16[768,3072]{1,0:T(8,128)(2,1)} async-done(((bf16[384,3072]{1,0:T(8,128)(2,1)}), bf16[768,3072]{1,0:T(8,128)(2,1)}) %all-gather.7.cloned.1.call-update) | async-done | bytes 4718608 | tf_op jit(solution)/shard_map/all_gather | solution.py:325
  40.6 52.1 %layer.1 = (bf16[256,768]{1,0:T(8,128)(2,1)}, f32[256,768]{1,0:T(8,128)}, bf16[256,768]{1,0:T(8,128)(2,1)}, bf16[256,1536]{1,0:T(8,128)(2,1)}, bf16[256,768]{1,0...) custom-call(s32[1]{0:T(128)S(6)} %copy.30.length_ref, ...), custom_call_target="tpu_custom_call" | custom-call | tf_op jit(solution)/shard_map/layer/pallas_call | solution.py:301
  92.7 2.2 pad_maximum_fusion
  95.0 2.2 convolution_convert_fusion.1
  97.4 3.6 convolution_convert_fusion
  101.1 3.6 reduce-scatter.6.cloned.1.call-done
  104.8 13.8 %reduce-scatter.8.cloned.1.call-done = bf16[768,768]{1,0:T(8,128)(2,1)} async-done(((bf16[1536,768]{1,0:T(8,128)(2,1)}), bf16[768,768]{1,0:T(8,128)(2,1)}) %reduce-scatter.8.cloned.1.call-update) | async-done | bytes 1179664 | tf_op jit(solution)/shard_map/reduce_scatter | solution.py:335
  118.6 16.5 %reduce-scatter.4.cloned.1.call-done = bf16[384,3072]{1,0:T(8,128)(2,1)} async-done(((bf16[768,3072]{1,0:T(8,128)(2,1)}), bf16[384,3072]{1,0:T(8,128)(2,1)}) %reduce-scatter.4.cloned.1.call-update) | async-done | bytes 2359312 | tf_op jit(solution)/shard_map/reduce_scatter | solution.py:335
  136.4 2.5 all-reduce
  139.0 42.5 %psum.28 = f32[384]{0:T(512)} all-reduce(f32[384]{0:T(512)S(1)} %dynamic-slice.1), channel_id=1, replica_groups=mesh['dp'=16,'fsdp'=2] {'dp'}, use_global_device_ids=true, to_apply=%region_1.0 | all-reduce | flops 384 | bytes 3072 | tf_op jit(solution)/shard_map/psum | solution.py:341
  181.5 68.7 %all-reduce.5.cloned.1.call-done = f32[152,768]{1,0:T(8,128)} async-done(((f32[152,768]{1,0:T(8,128)}), f32[152,768]{1,0:T(8,128)}) %all-reduce.5.cloned.1.call-update) | async-done | bytes 466960 | tf_op jit(solution)/shard_map/psum | solution.py:341
  250.2 1.6 slice.31
  256.0 1.7 slice_bitcast_fusion
  257.7 152.7 %all-reduce.7.cloned.1.call-done = (bf16[384,3072]{1,0:T(8,128)(2,1)}, bf16[768,768]{1,0:T(8,128)(2,1)}) async-done(((bf16[384,3072]{1,0:T(8,128)(2,1)}, bf16[768,768]{1,0:T(8,128)(2,1)}), (bf16[384,3072]{1,0:T(8,128)(2,1)}, bf16[768,768]{1,0:T(8,128)(2,1)})) %all-reduce.7.cloned.1.call-update) | async-done | bytes 3538960 | tf_op jit(solution)/shard_map/psum | solution.py:341
  410.4 4.5 %convert_element_type.13 = f32[384,3072]{1,0:T(8,128)} convert(bf16[384,3072]{1,0:T(8,128)(2,1)} %get-tuple-element.35) | non-fusion elementwise | flops 1179648 | bytes 7077888 | tf_op jit(solution)/shard_map/convert_element_type | solution.py:342
  414.9 1.6 convert_element_type.15
  (56 shorter events, 6.9 us)
Async XLA Ops:
  7.2 1.6 copy-start.5
  7.2 1.8 copy-start.10
  7.2 1.8 copy-start.11
  7.2 1.8 copy-start.12
  7.2 1.8 copy-start.13
  7.2 10.1 %copy-start.8 = (bf16[4,768]{1,0:T(4,128)(2,1)S(1)}, bf16[4,768]{1,0:T(4,128)(2,1)}, u32[]{:S(2)}) copy-start(bf16[4,768]{1,0:T(4,128)(2,1)} %param.18) | copy-start | bytes 18436
  7.2 12.1 %copy-start.7 = (bf16[16,768]{1,0:T(8,128)(2,1)S(1)}, bf16[16,768]{1,0:T(8,128)(2,1)}, u32[]{:S(2)}) copy-start(bf16[16,768]{1,0:T(8,128)(2,1)} %param.23) | copy-start | bytes 73732
  7.3 14.0 %copy-start.6 = (bf16[48,768]{1,0:T(8,128)(2,1)S(1)}, bf16[48,768]{1,0:T(8,128)(2,1)}, u32[]{:S(2)}) copy-start(bf16[48,768]{1,0:T(8,128)(2,1)} %param.21) | copy-start | bytes 221188
  7.3 18.4 %all-gather.9.cloned.1.call-start = ((), (), s32[]{:S(2)}) async-start(), calls=%async_computation.4 | async-start | bytes 3538944 | tf_op jit(solution)/shard_map/all_gather | solution.py:325
  8.0 32.6 %all-gather.7.cloned.1.call-start = ((), (), s32[]{:S(2)}) async-start(), calls=%async_computation.3 | async-start | bytes 7077888 | tf_op jit(solution)/shard_map/all_gather | solution.py:325
  8.7 96.0 %reduce-scatter.6.cloned.1.call-start = ((), (), s32[]{:S(2)}) async-start(), calls=%async_computation.6 | async-start | bytes 1400832 | tf_op jit(solution)/shard_map/reduce_scatter | solution.py:335
  92.7 2.3 copy-start.2
  92.7 2.3 copy-start.4
  95.0 23.7 %reduce-scatter.8.cloned.1.call-start = ((), (), s32[]{:S(2)}) async-start(), calls=%async_computation.8 | async-start | bytes 3538944 | tf_op jit(solution)/shard_map/reduce_scatter | solution.py:335
  95.0 2.3 copy-start
  95.0 2.3 copy-start.3
  97.3 37.8 %reduce-scatter.4.cloned.1.call-start = ((), (), s32[]{:S(2)}) async-start(), calls=%async_computation.5 | async-start | bytes 7077888 | tf_op jit(solution)/shard_map/reduce_scatter | solution.py:335
  101.0 34.2 %copy-start.14 = (u32[32]{0:T(128)S(1)}, u32[32]{0:T(128)}, u32[]{:S(2)}) copy-start(u32[32]{0:T(128)} %constant.5) | copy-start | bytes 388
  101.0 35.4 %copy-start.9 = (f32[1,768]{1,0:T(1,128)S(1)}, f32[1,768]{1,0:T(1,128)}, u32[]{:S(2)}) copy-start(f32[1,768]{1,0:T(1,128)} %get-tuple-element.24) | copy-start | bytes 9220
  101.0 149.2 %all-reduce.5.cloned.1.call-start = ((), (), s32[]{:S(2)}) async-start(), calls=%async_computation.7 | async-start | bytes 933888 | tf_op jit(solution)/shard_map/psum | solution.py:341
  104.8 305.6 %all-reduce.7.cloned.1.call-start = ((), (), s32[]{:S(2)}) async-start(), calls=%async_computation.9 | async-start | bytes 7077888 | tf_op jit(solution)/shard_map/psum | solution.py:341
  410.4 4.5 %copy-start.1 = (bf16[768,768]{1,0:T(8,128)(2,1)S(1)}, bf16[768,768]{1,0:T(8,128)(2,1)}, u32[]{:S(2)}) copy-start(bf16[768,768]{1,0:T(8,128)(2,1)} %get-tuple-element.36) | copy-start | bytes 3538948
Sparse Core Ops, SparseCore 0:
  9.6 13.7 all-gather.8
  25.0 15.5 all-gather.6
  95.1 9.6 reduce-scatter.5
  107.5 11.0 reduce-scatter.7
  121.3 13.7 reduce-scatter.3
  141.0 109.1 all-reduce.4
  255.9 154.3 all-reduce.6

commit v2 on v1

v2 whole, which is shorter than its diff:
```python
import functools
import types

import jax
import jax.numpy as jnp
from jax import lax
from jax.experimental import pallas as pl
from jax.experimental.pallas import tpu as pltpu
from jax.sharding import PartitionSpec as P

F32 = jnp.float32
BF16 = jnp.bfloat16
EPS = 1e-05
STEPS = 16
CHUNK = 256
PAD = 8
LOG2E = 1.4426950408889634
MB = 2**20
VMEM = pl.BlockSpec(memory_space=pltpu.VMEM)
SMEM = pl.BlockSpec(memory_space=pltpu.SMEM)
ANY = pl.BlockSpec(memory_space=pl.ANY)
MESH = pl.DeviceIdType.MESH


def dot(left, right, over=(1, 0)):
    dims = (((over[0],), (over[1],)), ((), ()))
    return lax.dot_general(left, right, dims, preferred_element_type=F32)


def span(index, size):
    return pl.ds(pl.multiple_of(index * size, size), size)


def repeat(count, step):
    def run(index, carry):
        step(index)
        return carry

    lax.fori_loop(0, count, run, 0)


def row_plan(s):
    bias = s.N + s.K
    return types.SimpleNamespace(conv=s.N, bias=bias, dt_bias=bias + 1, skip=bias + 2, gain=bias + 3)


def start_norm(s):
    def run(block):
        rows = span(block, 64)
        x = s.tok[rows, :].astype(F32)
        scale = lax.rsqrt(jnp.mean(x * x, axis=1, keepdims=True) + EPS)
        s.inv[rows, :] = jnp.broadcast_to(scale, (64, 128))
        at = block * 64 + lax.broadcasted_iota(jnp.int32, (64, 1), 0)
        live = (at < s.length[0]).astype(F32)
        s.d_branch[rows, :] = (live * s.cot[rows, :].astype(F32)).astype(BF16)

    repeat(s.T // 64, run)


def norm(s):
    def run(block):
        rows = span(block, 64)
        x = s.tok[rows, :].astype(F32)
        s.normed[rows, :] = (x * s.inv[rows, pl.ds(0, 1)] * s.gain[...]).astype(BF16)

    repeat(s.T // 64, run)


def project_inner(s, first, count):
    at = row_plan(s)

    def run(index):
        cols = span(first + index, 256)
        s.inner[pl.ds(PAD, s.T), cols] = dot(s.normed[...], s.w_in[:, cols])

    repeat(count, run)

    def convolve(index):
        cols = span(2 * first + index, 128)
        value = s.small[pl.ds(at.bias, 1), cols] + sum(
            s.small[pl.ds(at.conv + k, 1), cols] * s.inner[pl.ds(PAD - s.K + 1 + k, s.T), cols]
            for k in range(s.K)
        )
        sigma = jax.nn.sigmoid(value)
        s.active[:, cols] = (value * sigma).astype(BF16)
        s.cslope[:, cols] = sigma * (1.0 + value * (1.0 - sigma))

    repeat(2 * count, convolve)


def project_gate(s, first, count):
    def run(index):
        cols = span(first + index, 256)
        source = pl.ds(pl.multiple_of(s.E + (first + index) * 256, 256), 256)
        value = dot(s.normed[...], s.w_in[:, source])
        sigma = jax.nn.sigmoid(value)
        s.gact[:, cols] = value * sigma
        s.gslope[:, cols] = sigma * (1.0 + value * (1.0 - sigma))

    repeat(count, run)


def diagonal(s):
    wide = STEPS * s.N
    at = lax.broadcasted_iota(jnp.int32, (s.T, wide), 0)
    to = lax.broadcasted_iota(jnp.int32, (s.T, wide), 1)
    return (at % STEPS == to // s.N).astype(F32)


def spread_rows(s, source):
    ones = jnp.ones((STEPS, 128), BF16)
    wide = STEPS * s.N

    def run(block):
        s.spread[span(block, wide), :] = dot(source[span(block, STEPS), :], ones, (0, 0))

    repeat(s.T // STEPS, run)


def scan_inputs(s):
    wide = STEPS * s.N
    at = row_plan(s)
    s.proj[...] = dot(s.active[...], s.w_x[...]).astype(BF16)
    row = lax.broadcasted_iota(jnp.int32, (s.J, wide), 0)
    col = lax.broadcasted_iota(jnp.int32, (s.J, wide), 1)
    mask = diagonal(s)
    pick_b = (row == s.R + col % s.N).astype(BF16)
    pick_c = (row == s.R + s.N + col % s.N).astype(BF16)
    s.bmat[...] = (dot(s.proj[...], pick_b) * mask).astype(BF16)
    s.cmat[...] = (dot(s.proj[...], pick_c) * mask).astype(BF16)
    spread_rows(s, s.bmat)

    def run(index):
        cols = span(index, 256)
        pre = dot(s.proj[:, : s.R], s.w_dt[:, cols]) + s.small[pl.ds(at.dt_bias, 1), cols]
        size = jnp.maximum(pre, 0.0) + jnp.log1p(jnp.exp(-jnp.abs(pre)))
        s.step[:, cols] = size
        s.sigp[:, cols] = jax.nn.sigmoid(pre)
        s.drive[:, cols] = size * s.active[:, cols].astype(F32)

    repeat(s.E // 256, run)
    s.decay[...] = -jnp.exp(s.small[pl.ds(0, s.N), :]) * LOG2E


def forward_scan(s):
    N, E, wide = s.N, s.E, STEPS * s.N
    s.states[pl.ds(0, N), :] = jnp.zeros((N, E), BF16)

    def scan_sum(block):
        rows = span(block, STEPS)
        held = s.states[pl.ds(pl.multiple_of(block * wide + N, N), wide), :]
        s.mixed[rows, :] = dot(s.cmat[rows, :], held)

    def run(block, state):
        scan_sum(jnp.maximum(block - 1, 0))
        rows = span(block, STEPS)
        size, push = s.step[rows, :], s.drive[rows, :]
        for i in range(STEPS):
            t = block * STEPS + i
            b_row = s.spread[span(t, N), :]
            b_row = jnp.concatenate([b_row] * (E // 128), axis=1)
            factor = jnp.exp2(jnp.broadcast_to(size[i : i + 1], (N, E)) * s.decay[...])
            state = factor * state + b_row * jnp.broadcast_to(push[i : i + 1], (N, E))
            s.states[span(t + 1, N), :] = state.astype(BF16)
        return state

    lax.fori_loop(0, s.T // STEPS, run, jnp.zeros((N, E), F32))
    scan_sum(s.T // STEPS - 1)


def mix(s):
    at = row_plan(s)

    def run(index):
        cols = span(index, 128)
        value = s.mixed[pl.ds(0, s.T), cols] + s.small[pl.ds(at.skip, 1), cols] * s.active[:, cols].astype(F32)
        s.mixed[pl.ds(0, s.T), cols] = value
        s.gated[:, cols] = (value * s.gact[:, cols]).astype(BF16)

    repeat(s.E // 128, run)


def back_out(s):
    at = row_plan(s)

    def run(index):
        cols = span(index, 256)
        d_gated = dot(s.d_branch[...], s.w_out[cols, :], (1, 1))
        d_value = d_gated * s.gact[:, cols]
        s.d_mixed[:, cols] = d_value
        s.d_gate[:, cols] = (d_gated * s.mixed[pl.ds(0, s.T), cols] * s.gslope[:, cols]).astype(BF16)
        s.rows[pl.ds(at.skip, 1), cols] = jnp.sum(
            d_value * s.active[:, cols].astype(F32), axis=0, keepdims=True
        )

    repeat(s.E // 256, run)


def project_out(s):
    def run(index):
        cols = span(index, 256)
        branch = dot(s.gated[...], s.w_out[:, cols])
        at = lax.broadcasted_iota(jnp.int32, (s.T, 1), 0)
        live = (at < s.length[0]).astype(F32)
        s.output[:, cols] = (s.tok[:, cols].astype(F32) + live * branch).astype(BF16)

    repeat(s.D // 256, run)


def backward_scan(s, between=None):
    N, E, wide, half = s.N, s.E, STEPS * s.N, s.N // 2
    blocks = s.T // STEPS
    spread_rows(s, s.cmat)
    s.carry[...] = jnp.zeros((N, E), F32)
    s.rows[pl.ds(0, N), :] = jnp.zeros((N, E), F32)
    at = lax.broadcasted_iota(jnp.int32, (STEPS, STEPS * half), 0)
    to = lax.broadcasted_iota(jnp.int32, (STEPS, STEPS * half), 1)
    gather = (at == to // half).astype(BF16)

    def run(k):
        block = blocks - 1 - k
        rows = span(block, STEPS)
        for chunk in range(E // CHUNK):
            cols = pl.ds(chunk * CHUNK, CHUNK)
            later, total = s.carry[:, cols], s.rows[pl.ds(0, N), cols]
            size, d_value = s.step[rows, cols], s.d_mixed[rows, cols]
            rate = s.decay[:, cols]
            for i in reversed(range(STEPS)):
                t = block * STEPS + i
                dt = jnp.broadcast_to(size[i : i + 1], (N, CHUNK))
                c_row = s.spread[span(t, N), :]
                c_row = jnp.concatenate([c_row] * (CHUNK // 128), axis=1)
                lam = c_row * jnp.broadcast_to(d_value[i : i + 1], (N, CHUNK)) + later
                s.lam[pl.ds(i * N, N), cols] = lam.astype(BF16)
                later = jnp.exp2(dt * rate) * lam
                weighted = later * s.states[span(t, N), cols].astype(F32)
                total = total + weighted * dt
                part = weighted * rate
                part = part[:half] + part[half:]
                if i % 2 == 1:
                    odd = part
                else:
                    s.part[pl.ds(i * half, N), cols] = jnp.concatenate([part, odd], axis=0).astype(BF16)
            s.carry[:, cols] = later
            s.rows[pl.ds(0, N), cols] = total
            held = s.lam[:, cols]
            s.gact[rows, cols] = dot(s.bmat[rows, :], held)
            s.gslope[rows, cols] = dot(gather, s.part[:, cols])
            b_part = dot(s.drive[rows, cols].astype(BF16), held, (1, 1))
            after = s.states[pl.ds(pl.multiple_of(block * wide + N, N), wide), cols]
            c_part = dot(d_value.astype(BF16), after, (1, 1))
            if chunk == 0:
                s.db[rows, :] = b_part
                s.dc[rows, :] = c_part
            else:
                s.db[rows, :] += b_part
                s.dc[rows, :] += c_part
        if between is not None:
            between(k)

    repeat(blocks, run)
    s.rows[pl.ds(0, N), :] = s.rows[pl.ds(0, N), :] * s.decay[...] * (1.0 / LOG2E)


def back_step(s):
    at = row_plan(s)

    def run(index):
        cols = span(index, 128)
        wide = s.active[:, cols].astype(F32)
        adjoint = s.gact[:, cols]
        d_pre = (wide * adjoint + s.gslope[:, cols] * (1.0 / LOG2E)) * s.sigp[:, cols]
        s.rows[pl.ds(at.dt_bias, 1), cols] = jnp.sum(d_pre, axis=0, keepdims=True)
        s.d_pre_low[:, cols] = d_pre.astype(BF16)
        s.d_mixed[:, cols] = (
            s.d_mixed[:, cols] * s.small[pl.ds(at.skip, 1), cols] + s.step[:, cols] * adjoint
        )

    repeat(s.E // 128, run)


def back_proj(s):
    wide = STEPS * s.N
    row = lax.broadcasted_iota(jnp.int32, (wide, s.N), 0)
    col = lax.broadcasted_iota(jnp.int32, (wide, s.N), 1)
    pick = (row % s.N == col).astype(BF16)
    mask = diagonal(s)
    s.d_proj[:, pl.ds(0, s.R)] = dot(s.d_pre_low[...], s.w_dt[...], (1, 1)).astype(BF16)
    s.d_proj[:, pl.ds(s.R, s.N)] = dot((s.db[...] * mask).astype(BF16), pick).astype(BF16)
    s.d_proj[:, pl.ds(s.R + s.N, s.N)] = dot((s.dc[...] * mask).astype(BF16), pick).astype(BF16)


def back_conv(s):
    at = row_plan(s)
    s.mixed[pl.ds(s.T, PAD), :] = jnp.zeros((PAD, s.E), F32)
    first = at.gain + 1

    def run(index):
        cols = span(index, 128)
        s.rows[pl.ds(first, s.R), cols] = dot(s.proj[:, : s.R], s.d_pre_low[:, cols], (0, 0))
        s.rows[pl.ds(first + s.R, s.J), cols] = dot(s.d_proj[...], s.active[:, cols], (0, 0))
        d_active = s.d_mixed[:, cols] + dot(s.d_proj[...], s.w_x[cols, :], (1, 1))
        d_value = d_active * s.cslope[:, cols]
        s.mixed[pl.ds(0, s.T), cols] = d_value
        s.rows[pl.ds(at.bias, 1), cols] = jnp.sum(d_value, axis=0, keepdims=True)
        total = jnp.zeros_like(d_value)
        for k in range(s.K):
            s.rows[pl.ds(at.conv + k, 1), cols] = jnp.sum(
                d_value * s.inner[pl.ds(PAD - s.K + 1 + k, s.T), cols], axis=0, keepdims=True
            )
            taps = s.small[pl.ds(at.conv + k, 1), cols]
            total = total + taps * s.mixed[pl.ds(s.K - 1 - k, s.T), cols]
        s.d_inner[:, cols] = total.astype(BF16)

    repeat(s.E // 128, run)


def back_in(s):
    def run(index):
        rows = span(index, 256)
        s.d_normed[:, rows] = dot(s.d_inner[...], s.w_in[rows, pl.ds(0, s.E)], (1, 1)) + dot(
            s.d_gate[...], s.w_in[rows, pl.ds(s.E, s.E)], (1, 1)
        )

    repeat(s.D // 256, run)


def back_norm(s):
    s.d_gain[...] = jnp.zeros((1, s.D), F32)

    def run(block):
        rows = span(block, 64)
        x = s.tok[rows, :].astype(F32)
        scale = s.inv[rows, pl.ds(0, 1)]
        d_value = s.d_normed[rows, :]
        s.d_gain[...] += jnp.sum(d_value * x * scale, axis=0, keepdims=True)
        d_scaled = d_value * s.gain[...]
        shared = jnp.mean(d_scaled * x, axis=1, keepdims=True)
        s.input_grad[rows, :] = (
            s.cot[rows, :].astype(F32) + scale * d_scaled - x * (scale * scale * scale) * shared
        )

    repeat(s.T // 64, run)


def sizes(tokens, w_out, a_log, w_dt, w_x, conv_w):
    return dict(
        T=tokens.shape[0], D=tokens.shape[1], E=w_out.shape[0], N=a_log.shape[0],
        R=w_dt.shape[0], J=w_x.shape[1], K=conv_w.shape[0],
    )


def scratch_plan(z):
    T, D, E, N, R, J, K = (z[n] for n in "TDENRJK")
    wide = STEPS * N
    full, low = ((T, E), F32), ((T, E), BF16)
    padded = ((T + PAD, E), F32)
    count = N + K + 4
    return dict(
        inv=((T, 128), F32), gain=((1, D), F32), small=((count, E), F32), inner=padded, gact=full, gslope=full,
        cslope=full, active=low, proj=((T, J), BF16), bmat=((T, wide), BF16), cmat=((T, wide), BF16),
        spread=((T * N, 128), F32), decay=((N, E), F32), step=full, drive=full, sigp=full,
        mixed=padded, d_mixed=full, states=(((T + 1) * N, E), BF16), carry=((N, E), F32),
        lam=((wide, E), BF16), part=((wide // 2, E), BF16), db=((T, wide), F32), dc=((T, wide), F32),
        d_pre_low=low, d_proj=((T, J), BF16), d_normed=((T, D), F32), d_gain=((1, D), F32),
    )


def plain_kernel(z, names, *refs):
    s = types.SimpleNamespace(**z, **dict(zip(names, refs)))
    at = row_plan(s)
    s.small[pl.ds(0, s.N), :] = s.a_log[...].astype(F32)
    s.small[pl.ds(at.conv, s.K), :] = s.conv_w[...].astype(F32)
    s.small[pl.ds(at.bias, 1), :] = s.conv_b[...].astype(F32)
    s.small[pl.ds(at.dt_bias, 1), :] = s.dt_bias[...].astype(F32)
    s.small[pl.ds(at.skip, 1), :] = s.d_skip[...].astype(F32)
    s.gain[...] = s.gain_in[...].astype(F32)
    s.rows[...] = jnp.zeros(s.rows.shape, F32)
    s.inner[pl.ds(0, PAD), :] = jnp.zeros((PAD, s.E), F32)
    for step in (start_norm, norm):
        step(s)
    project_inner(s, 0, s.E // 256)
    project_gate(s, 0, s.E // 256)
    for step in (scan_inputs, forward_scan, mix, project_out, back_out):
        step(s)
    backward_scan(s)
    for step in (back_step, back_proj, back_conv, back_in, back_norm):
        step(s)
    s.g_gain[...] = s.d_gain[...]


def plain_layer(length, tokens, cotangent, gain, w_in, conv_w, conv_b, w_x, w_dt, dt_bias, a_log, d_skip, w_out):
    z = sizes(tokens, w_out, a_log, w_dt, w_x, conv_w)
    T, D, E, N, R, J, K = (z[n] for n in "TDENRJK")
    plan = scratch_plan(z)
    ins = ("length", "tok", "cot", "gain_in", "w_in", "conv_w", "conv_b", "w_x", "w_dt", "dt_bias", "a_log", "d_skip", "w_out")
    outs = dict(
        output=((T, D), BF16), input_grad=((T, D), F32), normed=((T, D), BF16), gated=((T, E), BF16),
        d_branch=((T, D), BF16), d_inner=((T, E), BF16), d_gate=((T, E), BF16), g_gain=((1, D), F32),
        rows=((N + K + 4 + R + J, E), F32),
    )
    names = list(ins) + list(outs) + list(plan)
    return pl.pallas_call(
        functools.partial(plain_kernel, z, names),
        out_shape=[jax.ShapeDtypeStruct(*spec) for spec in outs.values()],
        in_specs=[SMEM] + [VMEM] * 12,
        out_specs=[VMEM] * len(outs),
        scratch_shapes=[pltpu.VMEM(*spec) for spec in plan.values()],
        compiler_params=pltpu.CompilerParams(vmem_limit_bytes=60 * MB),
        name="plain_layer",
    )(length, tokens, cotangent, gain, w_in, conv_w, conv_b, w_x, w_dt, dt_bias, a_log, d_skip, w_out)


def plain_body(tokens, lengths, cotangent, *shards):
    axes = (0, 0, 1, 0, 0, 1, 0, 1, 0, 0)
    weights = [lax.all_gather(w, "fsdp", axis=a, tiled=True) for w, a in zip(shards, axes)]
    weights = [w.reshape(1, -1) if w.ndim == 1 else w for w in weights]
    output, input_grad, normed, gated, d_branch, d_inner, d_gate, g_gain, rows = plain_layer(
        lengths, tokens[0], cotangent[0], *weights
    )
    big_in = dot(normed, jnp.concatenate([d_inner, d_gate], axis=1), (0, 0))
    big_out = dot(gated, d_branch, (0, 0))

    def scatter(value, axis):
        return lax.psum_scatter(value, "fsdp", scatter_dimension=axis, tiled=True)

    own = (
        scatter(big_in.astype(BF16), 0), scatter(big_out.astype(BF16), 0),
        scatter(rows, 1), scatter(g_gain[0], 0),
    )
    own_in, own_out, rows, own_gain = lax.psum(own, "dp")
    N, K, R = shards[7].shape[0], shards[2].shape[0], shards[5].shape[0]
    M = N + K + 4
    return (
        output[None], input_grad[None], own_gain, own_in.astype(F32), rows[N : N + K], rows[N + K],
        rows[M + R :].T, rows[M : M + R], rows[N + K + 1], rows[:N], rows[N + K + 2], own_out.astype(F32),
    )


ORDERS = ((0, 1, 2, 3), (1, 0, 2, 3), (2, 0, 1, 3))
LEVELS = 4
PIECES = 2**LEVELS
GATHERS = 10
SWAPS = 6


def packed_rows(s):
    return s.N + s.K + 4


class Sum:
    def __init__(self, s, sem, order, acc, recv, out, first, piece):
        self.s, self.sem, self.order, self.piece = s, sem, order, piece
        self.acc, self.recv, self.out = acc, recv, out
        self.first, self.first_recv = first * PIECES * piece, first * (PIECES - 1) * piece
        self.bit = [lax.rem(s.dp // 2**b, 2) for b in order]

    def partner(self, level):
        b = self.order[level]
        return (self.s.dp + (1 - 2 * self.bit[level]) * 2**b, self.s.me)

    def rows(self, level, mine):
        start = 0
        for above in range(level):
            start = start + self.bit[above] * (PIECES >> (above + 1))
        bit = self.bit[level] if mine else 1 - self.bit[level]
        start = start + bit * (PIECES >> (level + 1))
        count = (PIECES >> (level + 1)) * self.piece
        return pl.multiple_of(self.first + start * self.piece, 16), count

    def landing(self, level):
        start = self.first_recv + (PIECES - (PIECES >> level)) * self.piece
        return start, (PIECES >> (level + 1)) * self.piece

    def reduce_copy(self, level):
        return self.s.remote(
            self.acc.at[pl.ds(*self.rows(level, False)), :],
            self.recv.at[pl.ds(*self.landing(level)), :],
            self.sem + level, self.partner(level),
        )

    def spread_copy(self, level, mine=True):
        rows = pl.ds(*self.rows(level, mine))
        return self.s.remote(
            self.out.at[rows, :], self.out.at[rows, :], self.sem + LEVELS + level, self.partner(level)
        )

    def start(self):
        self.reduce_copy(0).start()

    def reduce(self, level):
        self.reduce_copy(level).wait_recv()
        start, count = self.rows(level, True)
        landed = self.landing(level)[0]
        last = level == LEVELS - 1
        target = self.out if last else self.acc

        def add(index):
            here = pl.ds(pl.multiple_of(start + index * self.piece, 16), self.piece)
            there = pl.ds(pl.multiple_of(landed + index * self.piece, 16), self.piece)
            target[here, :] = (self.acc[here, :].astype(F32) + self.recv[there, :].astype(F32)).astype(BF16)

        repeat(count // self.piece, add)
        if last:
            self.spread_copy(level).start()
        else:
            self.reduce_copy(level + 1).start()

    def spread(self, level):
        self.spread_copy(level, False).wait_recv()
        if level > 0:
            self.spread_copy(level - 1).start()

    def finish(self):
        for level in range(LEVELS):
            self.reduce_copy(level).wait_send()
            self.spread_copy(level).wait_send()


def fused_kernel(z, names, *refs):
    s = types.SimpleNamespace(**z, **dict(zip(names, refs)))
    D, E = s.D, s.E
    DH, EH = D // 2, E // 2
    at = row_plan(s)
    count = packed_rows(s)
    s.dp, s.me = lax.axis_index("dp"), lax.axis_index("fsdp")
    other = 1 - s.me
    peer = (s.dp, other)

    def remote(src, dst, sem, device):
        return pltpu.make_async_remote_copy(
            src_ref=src, dst_ref=dst, send_sem=s.send.at[sem], recv_sem=s.recv_sem.at[sem],
            device_id=device, device_id_type=MESH,
        )

    s.remote = remote
    units = []
    for unit in range(3):
        for color in range(3):
            index = 3 * unit + color
            units.append(
                Sum(s, GATHERS + SWAPS + 2 * LEVELS * index, ORDERS[color], s.acc, s.recv, s.out, index, 16)
            )
    units.append(Sum(s, GATHERS + SWAPS + 2 * LEVELS * 9, ORDERS[0], s.acc_rows, s.recv_rows, s.out_rows, 0, 32))

    barrier = pltpu.get_barrier_semaphore()
    pl.semaphore_signal(barrier, inc=1, device_id=peer, device_id_type=MESH)
    for level in range(LEVELS):
        pl.semaphore_signal(barrier, inc=1, device_id=units[0].partner(level), device_id_type=MESH)

    mine_d, mine_e = span(s.me, DH), span(s.me, EH)
    theirs_d, theirs_e = span(other, DH), span(other, EH)
    local_in = pltpu.make_async_copy(s.w_in_own, s.w_in.at[mine_d, :], s.local.at[0])
    local_out = pltpu.make_async_copy(s.w_out_own, s.w_out.at[mine_e, :], s.local.at[1])
    local_in.start()
    local_out.start()
    s.pack[pl.ds(0, s.N), :] = s.a_log[...].astype(F32)
    s.pack[pl.ds(at.conv, s.K), :] = s.conv_w[...].astype(F32)
    s.pack[pl.ds(at.bias, 1), :] = s.conv_b[...].astype(F32)
    s.pack[pl.ds(at.dt_bias, 1), :] = s.dt_bias[...].astype(F32)
    s.pack[pl.ds(at.skip, 1), :] = s.d_skip[...].astype(F32)
    s.pack[pl.ds(at.gain, 1), :] = jnp.zeros((1, EH), F32)
    s.pack[pl.ds(at.gain, 1), pl.ds(0, DH)] = s.gain_own[...].astype(F32)
    pl.semaphore_wait(barrier, LEVELS + 1)

    width = 2 * E // 6
    gathers = [remote(s.pack, s.pack_in, 0, peer)]
    for j in range(6):
        cols = pl.ds(j * width, width)
        gathers.append(remote(s.w_in_own.at[:, cols], s.w_in.at[mine_d, cols], 1 + j, peer))
    gathers.append(remote(s.w_x_own, s.w_x.at[mine_e, :], 7, peer))
    gathers.append(remote(s.w_dt_own, s.w_dt_in, 8, peer))
    gathers.append(remote(s.w_out_own, s.w_out.at[mine_e, :], 9, peer))
    for copy in gathers:
        copy.start()

    swaps = [
        remote(s.normed.at[:, theirs_d], s.normed_in, GATHERS, peer),
        remote(s.d_branch, s.d_branch_in, GATHERS + 1, peer),
        remote(s.gated.at[:, theirs_e], s.gated_in, GATHERS + 2, peer),
        remote(s.d_gate, s.d_gate_in, GATHERS + 3, peer),
        remote(s.d_inner, s.d_inner_in, GATHERS + 4, peer),
        remote(s.rows.at[:, theirs_e], s.rows_in, GATHERS + 5, peer),
    ]

    start_norm(s)
    swaps[1].start()
    s.w_x[mine_e, :] = s.w_x_own[...]
    s.w_dt[:, mine_e] = s.w_dt_own[...]
    s.small[:, mine_e] = s.pack[...]
    s.gain[:, mine_d] = s.pack[pl.ds(at.gain, 1), pl.ds(0, DH)]
    s.inner[pl.ds(0, PAD), :] = jnp.zeros((PAD, E), F32)
    gathers[0].wait_recv()
    s.small[:, theirs_e] = s.pack_in[...]
    s.gain[:, theirs_d] = s.pack_in[pl.ds(at.gain, 1), pl.ds(0, DH)]
    norm(s)
    swaps[0].start()
    local_in.wait()
    for j in range(3):
        gathers[1 + j].wait_recv()
        project_inner(s, 2 * j, 2)
    gathers[7].wait_recv()
    gathers[8].wait_recv()
    s.w_dt[:, theirs_e] = s.w_dt_in[...]
    scan_inputs(s)
    for j in range(3):
        gathers[4 + j].wait_recv()
        project_gate(s, 2 * j, 2)
    forward_scan(s)
    mix(s)
    swaps[2].start()
    local_out.wait()
    gathers[9].wait_recv()
    back_out(s)
    swaps[3].start()
    project_out(s)

    def product(left, left_in, right, right_in, shift, cols, across):
        own = pl.ds(pl.multiple_of(shift + cols.start, 128), cols.size)
        total = dot(left[:, own], right[:, across], (0, 0)) + dot(left_in[:, cols], right_in[:, across], (0, 0))
        return total.astype(BF16)

    def grad_out(color):
        cols = pl.ds(256 * color, 256)
        s.acc[pl.ds(256 * color, 256), :] = product(
            s.gated, s.gated_in, s.d_branch, s.d_branch_in, s.me * EH, cols, pl.ds(0, D)
        )

    def grad_in(unit, color, right, right_in):
        first = 256 * (3 * unit + color)
        parts = (((0, 256, 0),), ((256, 128, 0), (0, 128, EH)), ((128, 256, EH),))[color]
        for start, size, across in parts:
            s.acc[pl.ds(first, size), :] = product(
                s.normed, s.normed_in, right, right_in, s.me * DH, pl.ds(start, size), pl.ds(across, EH)
            )
            first += size

    swaps[1].wait_recv()
    swaps[2].wait_recv()
    for color in range(3):
        grad_out(color)
        units[color].start()
    swaps[0].wait_recv()
    swaps[3].wait_recv()
    for color in range(3):
        grad_in(1, color, s.d_gate, s.d_gate_in)
        units[3 + color].start()

    def event(unit, step):
        members = units[9:] if unit == 3 else units[3 * unit : 3 * unit + 3]
        for member in members:
            if step < LEVELS:
                member.reduce(step)
            else:
                member.spread(2 * LEVELS - 1 - step)

    schedule = {6: (0, 0), 10: (1, 0), 12: (0, 1), 14: (1, 1), 15: (0, 2)}

    def between(k):
        for when, what in schedule.items():
            pl.when(k == when)(functools.partial(event, *what))

    s.rows[pl.ds(at.gain, 1), :] = jnp.zeros((1, E), F32)
    backward_scan(s, between)
    event(1, 2)
    back_step(s)
    event(0, 3)
    back_proj(s)
    event(1, 3)
    back_conv(s)
    swaps[4].start()
    event(0, 4)
    event(1, 4)
    back_in(s)
    event(0, 5)
    event(1, 5)
    back_norm(s)
    s.rows[pl.ds(at.gain, 1), pl.ds(0, DH)] = s.d_gain[:, pl.ds(0, DH)]
    s.rows[pl.ds(at.gain, 1), pl.ds(EH, DH)] = s.d_gain[:, pl.ds(DH, DH)]
    swaps[5].start()
    swaps[4].wait_recv()
    for color in range(3):
        grad_in(2, color, s.d_inner, s.d_inner_in)
        units[6 + color].start()
    swaps[5].wait_recv()
    total = s.rows.shape[0]
    s.acc_rows[...] = jnp.zeros(s.acc_rows.shape, BF16)
    for part in range(3):
        own = pl.ds(pl.multiple_of(s.me * EH + 256 * part, 128), 256)
        value = s.rows[:, own] + s.rows_in[:, pl.ds(256 * part, 256)]
        value = jnp.concatenate([value, jnp.zeros((160 - total, 256), F32)], axis=0)
        s.acc_rows[pl.ds(160 * part, 160), :] = value.astype(BF16)
    units[9].start()
    event(0, 6)
    event(1, 6)
    event(2, 0)
    event(3, 0)
    event(0, 7)
    event(1, 7)
    for step in range(1, 2 * LEVELS):
        event(2, step)
        event(3, step)
    for copy in gathers + swaps:
        copy.wait_send()
    for unit in units:
        unit.finish()


def fused_layer(length, tokens, cotangent, gain, w_in, conv_w, conv_b, w_x, w_dt, dt_bias, a_log, d_skip, w_out):
    z = sizes(tokens, jax.ShapeDtypeStruct((2 * w_out.shape[0], w_out.shape[1]), BF16), a_log, w_dt, w_x, conv_w)
    T, D, E, N, R, J, K = (z[n] for n in "TDENRJK")
    DH, EH = D // 2, E // 2
    total = N + K + 4 + R + J
    names = ("length", "tok", "cot", "gain_own", "w_in_own", "conv_w", "conv_b", "w_x_own", "w_dt_own", "dt_bias", "a_log", "d_skip", "w_out_own")
    outs = dict(
        output=((T, D), BF16), input_grad=((T, D), F32), out=((9 * 256, D), BF16), out_rows=((512, 256), BF16)
    )
    plan = scratch_plan(z)
    plan.update(
        w_in=((D, 2 * E), BF16), w_out=((E, D), BF16), w_x=((E, J), BF16), w_dt=((R, E), BF16),
        pack=((N + K + 4, EH), F32), pack_in=((N + K + 4, EH), F32), w_dt_in=((R, EH), BF16),
        normed=((T, D), BF16), gated=((T, E), BF16), d_branch=((T, D), BF16), d_inner=((T, E), BF16),
        d_gate=((T, E), BF16), rows=((total, E), F32), normed_in=((T, DH), BF16), d_branch_in=((T, D), BF16),
        gated_in=((T, EH), BF16), d_gate_in=((T, E), BF16), d_inner_in=((T, E), BF16), rows_in=((total, EH), F32),
        acc=((9 * 256, D), BF16), recv=((9 * 240, D), BF16), acc_rows=((512, 256), BF16), recv_rows=((480, 256), BF16),
    )
    sems = GATHERS + SWAPS + 2 * LEVELS * 10
    names = list(names) + list(outs) + list(plan) + ["local", "send", "recv_sem"]
    specs = [SMEM] + [VMEM] * 12
    specs[4] = specs[12] = ANY
    return pl.pallas_call(
        functools.partial(fused_kernel, z, names),
        out_shape=[jax.ShapeDtypeStruct(*spec) for spec in outs.values()],
        in_specs=specs,
        out_specs=[VMEM] * len(outs),
        scratch_shapes=[pltpu.VMEM(*spec) for spec in plan.values()]
        + [pltpu.SemaphoreType.DMA((2,)), pltpu.SemaphoreType.DMA((sems,)), pltpu.SemaphoreType.DMA((sems,))],
        compiler_params=pltpu.CompilerParams(collective_id=0, has_side_effects=True, vmem_limit_bytes=63 * MB),
        name="layer",
    )(length, tokens, cotangent, gain, w_in, conv_w, conv_b, w_x, w_dt, dt_bias, a_log, d_skip, w_out)


def finish_kernel(N, K, R, J, out, out_rows, output_in, grad_in_in, output, input_grad, *grads):
    g_gain, g_in, g_conv_w, g_conv_b, g_x, g_dt, g_dt_bias, g_a_log, g_skip, g_out = grads
    output[...] = output_in[...]
    input_grad[...] = grad_in_in[...]
    DH, D = g_in.shape[0], out.shape[1]
    g_out[...] = out[pl.ds(0, D), :].astype(F32)
    for place, unit in enumerate((2, 1)):
        for half in range(2):
            g_in[:, pl.ds((2 * place + half) * D, D)] = out[pl.ds(unit * D + half * DH, DH), :].astype(F32)
    M = N + K + 4
    for part in range(3):
        value = out_rows[pl.ds(160 * part, 160), :].astype(F32)
        cols = pl.ds(256 * part, 256)
        g_a_log[:, cols] = value[:N]
        g_conv_w[:, cols] = value[N : N + K]
        g_conv_b[:, cols] = value[N + K : N + K + 1]
        g_dt_bias[:, cols] = value[N + K + 1 : N + K + 2]
        g_skip[:, cols] = value[N + K + 2 : N + K + 3]
        row = value[N + K + 3 : N + K + 4]
        if part == 0:
            g_gain[:, pl.ds(0, 256)] = row
        elif part == 1:
            g_gain[:, pl.ds(256, DH - 256)] = row[:, : DH - 256]
        g_dt[:, cols] = value[M : M + R]
        turned = jnp.concatenate([value[M + R : M + R + J], jnp.zeros((128 - J, 256), F32)], axis=0).T
        g_x[cols, :] = turned[:, :J]


def fused_body(tokens, lengths, cotangent, *shards):
    shards = [w.reshape(1, -1) if w.ndim == 1 else w for w in shards]
    output, input_grad, out, out_rows = fused_layer(lengths, tokens[0], cotangent[0], *shards)
    gain, w_in, conv_w, conv_b, w_x, w_dt, dt_bias, a_log, d_skip, w_out = shards
    results = pl.pallas_call(
        functools.partial(finish_kernel, a_log.shape[0], conv_w.shape[0], w_dt.shape[0], w_x.shape[1]),
        out_shape=[jax.ShapeDtypeStruct(x.shape, x.dtype) for x in (output, input_grad)]
        + [jax.ShapeDtypeStruct(w.shape, F32) for w in shards],
        in_specs=[VMEM] * 4,
        out_specs=[VMEM] * 12,
        compiler_params=pltpu.CompilerParams(vmem_limit_bytes=60 * MB),
        name="finish",
    )(out, out_rows, output, input_grad)
    output, input_grad, *grads = results
    vectors = (0, 3, 6, 8)
    grads = [g.reshape(-1) if i in vectors else g for i, g in enumerate(grads)]
    return (output[None], input_grad[None], *grads)


def solution(mesh):
    seq, row, col, one = P(("dp", "fsdp"), None, None), P("fsdp", None), P(None, "fsdp"), P("fsdp")
    fused = mesh.shape["dp"] == PIECES and mesh.shape["fsdp"] == 2
    return jax.shard_map(
        fused_body if fused else plain_body,
        mesh=mesh,
        in_specs=(seq, P(("dp", "fsdp")), seq, one, row, col, one, row, col, one, col, one, row),
        out_specs=(seq, seq, one, row, col, one, row, col, one, col, one, row),
        check_vma=False,
    )
```

time: 424 us -> 151 us (0.36)
  waiting for transfers between devices: 272 us -> 0 us
  Pallas kernels: 52.1 us -> 135 us
  blocking collectives: 60.9 us -> 0 us
  between operations: 15.7 us -> 1.3 us
  matrix products: 5.85 us -> 0 us
    psum x2 -> x0, waiting for transfers between devices: 221 us -> none  [reduce_plain(): own_in, own_out, own_rows, own_gain = lax.psum(own, 'dp')]
    pallas_call x1 -> x2, Pallas kernels: 52.1 us -> 135 us  [the longest x1 129 us: fused_layer(): pl.pallas_call(functools.partial(fused_kernel, z, names), out_shape=[jax....]
    psum x1 -> x0, blocking collectives: 42.5 us -> none  [reduce_plain(): own_in, own_out, own_rows, own_gain = lax.psum(own, 'dp')]
    reduce_scatter x3 -> x0, waiting for transfers between devices: 34 us -> none  [scatter(): return lax.psum_scatter(value, 'fsdp', scatter_dimension=axis, tiled=True)]
    all_gather x8 -> x0, blocking collectives: 15.9 us -> none  [gather(): lax.all_gather(w, 'fsdp', axis=a, tiled=True)]
    all_gather x2 -> x0, waiting for transfers between devices: 14.9 us -> none  [gather(): lax.all_gather(w, 'fsdp', axis=a, tiled=True)]
    convert_element_type x2 -> x0, other arithmetic: 6.09 us -> none  [reduce_plain(): return (own_in.astype(F32), own_out.astype(F32), own_rows, own_gain)]
    dot_general x2 -> x0, matrix products: 5.85 us -> none  [the longest x1 3.61 us: reduce_plain(): lax.dot_general(normed, d_joined, (((0,), (0,)), ((), ())), preferred_ele...]
  transfers between devices with their start and end apart: 7 -> 0, of which waited for: 6 -> 0; matrix products, arithmetic and copies ran while one was open for 3% -> 0% of each run, Pallas kernels for 0% -> 0%
where the time goes in v2:
time: 151 us; the launch traced here: 150 us
  Pallas kernels  135 us (89%)
  local copies, waits for them, and re-layouts  8.59 us (6%)
  other arithmetic  5.12 us (3%)
    pallas_call x1, Pallas kernels, fused_layer(): pl.pallas_call(functools.partial(fused_kernel, z, names), out_shape=[jax....  129 us
    pallas_call x1, Pallas kernels, fused_body(): pl.pallas_call(functools.partial(finish_kernel, a_log.shape[0], conv_w.sh...  6.06 us
    pallas_call x4, other arithmetic, fused_body(): pl.pallas_call(functools.partial(finish_kernel, a_log.shape[0], conv_w.sh...  5.12 us
    reshape x4, local copies, waits for them, and re-layouts, fused_body(): shards = [w.reshape(1, -1) if w.ndim == 1 else w for w in shards]  5.03 us
    unnamed x2, local copies, waits for them, and re-layouts  3.56 us

profile of v2, /device:TPU:0, one launch (start us, length us, event | category | flops | bytes accessed | tf_op | source)
XLA Modules:
  0.0 150.1 jit_solution(5834151430334928107)
XLA Ops:
  1.3 1.2 reshape.48.refs_3_
  2.5 1.3 reshape.49.refs_6_
  3.8 1.3 reshape.50.refs_9_
  5.1 1.3 reshape.51.refs_11_
  6.3 1.7 %copy.25.refs_7_ = bf16[768,80]{1,0:T(8,128)(2,1)} copy(bf16[768,80]{0,1:T(8,128)(2,1)} %param.20) | data formatting | bytes 245760 | tf_op args[7]
  8.0 129.0 %layer.1 = (bf16[256,768]{1,0:T(8,128)(2,1)}, f32[256,768]{1,0:T(8,128)}, bf16[2304,768]{1,0:T(8,128)(2,1)}, bf16[512,256]{1,0:T(8,128)(2,1)}) custom-call(s32[1]{0:T(128)S(6)} %copy.27.refs_0_, bf16[256,768]{1,0:T(8,128)(2,1)} %bitcast.4, bf16[256,768]{1,0:T(8,128)(2,1)} %bitcast.5, bf16[1,384]{1,0:T(2,128)(2,1)} %reshape.48.refs_3_, ...), custom_call_target="tpu_custom_call" | custom-call | tf_op jit(solution)/shard_map/layer/pallas_call | solution.py:731
  137.1 6.1 %finish.1 = (bf16[256,768]{1,0:T(8,128)(2,1)}, f32[256,768]{1,0:T(8,128)}, f32[1,384]{1,0:T(1,128)}, f32[384,3072]{1,0:T(8,128)}, f32[4,768]{1,0:T(4,128)}, /*in...) custom-call(bf16[2304,768]{1,0:T(8,128)(2,1)} %get-tuple-element.28., ...), custom_call_target="tpu_custom_call" | custom-call | tf_op jit(solution)/shard_map/finish/pallas_call | solution.py:775
  143.1 1.3 reduce
  144.4 1.3 reduce.1
  145.7 1.3 reduce.2
  147.0 1.3 reduce.3
  148.3 1.8 %copy.26 = f32[768,80]{0,1:T(8,128)} copy(f32[768,80]{1,0:T(8,128)} %get-tuple-element.50) | data formatting | bytes 491520

commit v3 on v2

--- a/solution.py
+++ b/solution.py
@@ -107,12 +107,21 @@
     return (at % STEPS == to // s.N).astype(F32)
 
 
-def spread_rows(s, source):
-    ones = jnp.ones((STEPS, 128), BF16)
-    wide = STEPS * s.N
+def spread_rows(s):
+    N, J, wide = s.N, s.J, STEPS * s.N
+    state = lax.broadcasted_iota(jnp.int32, (N, J), 0)
+    col = lax.broadcasted_iota(jnp.int32, (N, J), 1)
+    mask = jnp.logical_or(col == s.R + state, col == s.R + N + state).astype(F32)
+    row = lax.broadcasted_iota(jnp.int32, (J, 256), 0)
+    lane = lax.broadcasted_iota(jnp.int32, (J, 256), 1)
+    first = jnp.logical_and(row < s.R + N, lane < 128)
+    last = jnp.logical_and(row >= s.R + N, lane >= 128)
+    ones = jnp.logical_or(first, last).astype(BF16)
 
     def run(block):
-        s.spread[span(block, wide), :] = dot(source[span(block, STEPS), :], ones, (0, 0))
+        rows = s.proj[span(block, STEPS), :].astype(F32)
+        parts = [(jnp.broadcast_to(rows[i : i + 1], (N, J)) * mask).astype(BF16) for i in range(STEPS)]
+        s.spread[span(block, wide), :] = dot(jnp.concatenate(parts, axis=0), ones)
 
     repeat(s.T // STEPS, run)
 
@@ -120,7 +129,7 @@
 def scan_inputs(s):
     wide = STEPS * s.N
     at = row_plan(s)
-    s.proj[...] = dot(s.active[...], s.w_x[...]).astype(BF16)
+    s.proj[...] = dot(s.active[...], s.w_xt[...], (1, 1)).astype(BF16)
     row = lax.broadcasted_iota(jnp.int32, (s.J, wide), 0)
     col = lax.broadcasted_iota(jnp.int32, (s.J, wide), 1)
     mask = diagonal(s)
@@ -128,7 +137,7 @@
     pick_c = (row == s.R + s.N + col % s.N).astype(BF16)
     s.bmat[...] = (dot(s.proj[...], pick_b) * mask).astype(BF16)
     s.cmat[...] = (dot(s.proj[...], pick_c) * mask).astype(BF16)
-    spread_rows(s, s.bmat)
+    spread_rows(s)
 
     def run(index):
         cols = span(index, 256)
@@ -136,7 +145,6 @@
         size = jnp.maximum(pre, 0.0) + jnp.log1p(jnp.exp(-jnp.abs(pre)))
         s.step[:, cols] = size
         s.sigp[:, cols] = jax.nn.sigmoid(pre)
-        s.drive[:, cols] = size * s.active[:, cols].astype(F32)
 
     repeat(s.E // 256, run)
     s.decay[...] = -jnp.exp(s.small[pl.ds(0, s.N), :]) * LOG2E
@@ -154,10 +162,11 @@
     def run(block, state):
         scan_sum(jnp.maximum(block - 1, 0))
         rows = span(block, STEPS)
-        size, push = s.step[rows, :], s.drive[rows, :]
+        size = s.step[rows, :]
+        push = size * s.active[rows, :].astype(F32)
         for i in range(STEPS):
             t = block * STEPS + i
-            b_row = s.spread[span(t, N), :]
+            b_row = s.spread[span(t, N), pl.ds(0, 128)]
             b_row = jnp.concatenate([b_row] * (E // 128), axis=1)
             factor = jnp.exp2(jnp.broadcast_to(size[i : i + 1], (N, E)) * s.decay[...])
             state = factor * state + b_row * jnp.broadcast_to(push[i : i + 1], (N, E))
@@ -210,7 +219,6 @@
 def backward_scan(s, between=None):
     N, E, wide, half = s.N, s.E, STEPS * s.N, s.N // 2
     blocks = s.T // STEPS
-    spread_rows(s, s.cmat)
     s.carry[...] = jnp.zeros((N, E), F32)
     s.rows[pl.ds(0, N), :] = jnp.zeros((N, E), F32)
     at = lax.broadcasted_iota(jnp.int32, (STEPS, STEPS * half), 0)
@@ -228,7 +236,7 @@
             for i in reversed(range(STEPS)):
                 t = block * STEPS + i
                 dt = jnp.broadcast_to(size[i : i + 1], (N, CHUNK))
-                c_row = s.spread[span(t, N), :]
+                c_row = s.spread[span(t, N), pl.ds(128, 128)]
                 c_row = jnp.concatenate([c_row] * (CHUNK // 128), axis=1)
                 lam = c_row * jnp.broadcast_to(d_value[i : i + 1], (N, CHUNK)) + later
                 s.lam[pl.ds(i * N, N), cols] = lam.astype(BF16)
@@ -246,7 +254,8 @@
             held = s.lam[:, cols]
             s.gact[rows, cols] = dot(s.bmat[rows, :], held)
             s.gslope[rows, cols] = dot(gather, s.part[:, cols])
-            b_part = dot(s.drive[rows, cols].astype(BF16), held, (1, 1))
+            drive = (size * s.active[rows, cols].astype(F32)).astype(BF16)
+            b_part = dot(drive, held, (1, 1))
             after = s.states[pl.ds(pl.multiple_of(block * wide + N, N), wide), cols]
             c_part = dot(d_value.astype(BF16), after, (1, 1))
             if chunk == 0:
@@ -299,7 +308,7 @@
         cols = span(index, 128)
         s.rows[pl.ds(first, s.R), cols] = dot(s.proj[:, : s.R], s.d_pre_low[:, cols], (0, 0))
         s.rows[pl.ds(first + s.R, s.J), cols] = dot(s.d_proj[...], s.active[:, cols], (0, 0))
-        d_active = s.d_mixed[:, cols] + dot(s.d_proj[...], s.w_x[cols, :], (1, 1))
+        d_active = s.d_mixed[:, cols] + dot(s.d_proj[...], s.w_xt[:, cols])
         d_value = d_active * s.cslope[:, cols]
         s.mixed[pl.ds(0, s.T), cols] = d_value
         s.rows[pl.ds(at.bias, 1), cols] = jnp.sum(d_value, axis=0, keepdims=True)
@@ -343,10 +352,10 @@
     repeat(s.T // 64, run)
 
 
-def sizes(tokens, w_out, a_log, w_dt, w_x, conv_w):
+def sizes(tokens, w_out, a_log, w_dt, w_xt, conv_w):
     return dict(
         T=tokens.shape[0], D=tokens.shape[1], E=w_out.shape[0], N=a_log.shape[0],
-        R=w_dt.shape[0], J=w_x.shape[1], K=conv_w.shape[0],
+        R=w_dt.shape[0], J=w_xt.shape[0], K=conv_w.shape[0],
     )
 
 
@@ -359,7 +368,7 @@
     return dict(
         inv=((T, 128), F32), gain=((1, D), F32), small=((count, E), F32), inner=padded, gact=full, gslope=full,
         cslope=full, active=low, proj=((T, J), BF16), bmat=((T, wide), BF16), cmat=((T, wide), BF16),
-        spread=((T * N, 128), F32), decay=((N, E), F32), step=full, drive=full, sigp=full,
+        spread=((T * N, 256), F32), decay=((N, E), F32), step=full, sigp=full,
         mixed=padded, d_mixed=full, states=(((T + 1) * N, E), BF16), carry=((N, E), F32),
         lam=((wide, E), BF16), part=((wide // 2, E), BF16), db=((T, wide), F32), dc=((T, wide), F32),
         d_pre_low=low, d_proj=((T, J), BF16), d_normed=((T, D), F32), d_gain=((1, D), F32),
@@ -389,11 +398,11 @@
     s.g_gain[...] = s.d_gain[...]
 
 
-def plain_layer(length, tokens, cotangent, gain, w_in, conv_w, conv_b, w_x, w_dt, dt_bias, a_log, d_skip, w_out):
-    z = sizes(tokens, w_out, a_log, w_dt, w_x, conv_w)
+def plain_layer(length, tokens, cotangent, gain, w_in, conv_w, conv_b, w_xt, w_dt, dt_bias, a_log, d_skip, w_out):
+    z = sizes(tokens, w_out, a_log, w_dt, w_xt, conv_w)
     T, D, E, N, R, J, K = (z[n] for n in "TDENRJK")
     plan = scratch_plan(z)
-    ins = ("length", "tok", "cot", "gain_in", "w_in", "conv_w", "conv_b", "w_x", "w_dt", "dt_bias", "a_log", "d_skip", "w_out")
+    ins = ("length", "tok", "cot", "gain_in", "w_in", "conv_w", "conv_b", "w_xt", "w_dt", "dt_bias", "a_log", "d_skip", "w_out")
     outs = dict(
         output=((T, D), BF16), input_grad=((T, D), F32), normed=((T, D), BF16), gated=((T, E), BF16),
         d_branch=((T, D), BF16), d_inner=((T, E), BF16), d_gate=((T, E), BF16), g_gain=((1, D), F32),
@@ -408,13 +417,14 @@
         scratch_shapes=[pltpu.VMEM(*spec) for spec in plan.values()],
         compiler_params=pltpu.CompilerParams(vmem_limit_bytes=60 * MB),
         name="plain_layer",
-    )(length, tokens, cotangent, gain, w_in, conv_w, conv_b, w_x, w_dt, dt_bias, a_log, d_skip, w_out)
+    )(length, tokens, cotangent, gain, w_in, conv_w, conv_b, w_xt, w_dt, dt_bias, a_log, d_skip, w_out)
 
 
 def plain_body(tokens, lengths, cotangent, *shards):
     axes = (0, 0, 1, 0, 0, 1, 0, 1, 0, 0)
     weights = [lax.all_gather(w, "fsdp", axis=a, tiled=True) for w, a in zip(shards, axes)]
     weights = [w.reshape(1, -1) if w.ndim == 1 else w for w in weights]
+    weights[4] = weights[4].T
     output, input_grad, normed, gated, d_branch, d_inner, d_gate, g_gain, rows = plain_layer(
         lengths, tokens[0], cotangent[0], *weights
     )
@@ -437,7 +447,21 @@
     )
 
 
-ORDERS = ((0, 1, 2, 3), (1, 0, 2, 3), (2, 0, 1, 3))
+ORDERS = (
+    (0, 1, 2, 3), (1, 0, 3, 2), (3, 1, 0, 2), (0, 1, 2, 3), (1, 0, 3, 2),
+    (2, 0, 1, 3), (1, 0, 3, 2), (2, 0, 1, 3), (0, 1, 2, 3), (1, 0, 2, 3),
+)
+DURING = {
+    5: ((0, 0), (1, 0)), 10: ((3, 0), (4, 0), (2, 0), (5, 0)), 12: ((1, 1),), 13: ((0, 1),),
+    15: ((4, 1), (3, 1)), 17: ((1, 2), (0, 2)), 18: ((5, 1), (2, 1), (3, 2), (4, 2)), 19: ((1, 3), (0, 3)),
+}
+AFTER = (
+    (5, 2), (2, 2), (3, 3), (4, 3), (1, 4), (0, 4), (6, 0), (8, 0), (7, 0), (5, 3), (2, 3), (3, 4), (4, 4), (9, 0),
+    (6, 1), (0, 5), (1, 5), (8, 1), (7, 1), (5, 4), (2, 4), (3, 5), (9, 1), (0, 6), (4, 5), (1, 6), (7, 2), (2, 5),
+    (5, 5), (6, 2), (8, 2), (9, 2), (3, 6), (7, 3), (6, 3), (8, 3), (0, 7), (9, 3), (6, 4), (7, 4), (4, 6), (1, 7),
+    (8, 4), (9, 4), (5, 6), (2, 6), (6, 5), (8, 5), (7, 5), (9, 5), (3, 7), (4, 7), (5, 7), (6, 6), (8, 6), (7, 6),
+    (9, 6), (6, 7), (8, 7), (2, 7), (7, 7), (9, 7),
+)
 LEVELS = 4
 PIECES = 2**LEVELS
 GATHERS = 10
@@ -539,9 +563,9 @@
         for color in range(3):
             index = 3 * unit + color
             units.append(
-                Sum(s, GATHERS + SWAPS + 2 * LEVELS * index, ORDERS[color], s.acc, s.recv, s.out, index, 16)
+                Sum(s, GATHERS + SWAPS + 2 * LEVELS * index, ORDERS[index], s.acc, s.recv, s.out, index, 16)
             )
-    units.append(Sum(s, GATHERS + SWAPS + 2 * LEVELS * 9, ORDERS[0], s.acc_rows, s.recv_rows, s.out_rows, 0, 32))
+    units.append(Sum(s, GATHERS + SWAPS + 2 * LEVELS * 9, ORDERS[9], s.acc_rows, s.recv_rows, s.out_rows, 0, 32))
 
     barrier = pltpu.get_barrier_semaphore()
     pl.semaphore_signal(barrier, inc=1, device_id=peer, device_id_type=MESH)
@@ -556,11 +580,11 @@
     local_out.start()
     s.pack[pl.ds(0, s.N), :] = s.a_log[...].astype(F32)
     s.pack[pl.ds(at.conv, s.K), :] = s.conv_w[...].astype(F32)
-    s.pack[pl.ds(at.bias, 1), :] = s.conv_b[...].astype(F32)
-    s.pack[pl.ds(at.dt_bias, 1), :] = s.dt_bias[...].astype(F32)
-    s.pack[pl.ds(at.skip, 1), :] = s.d_skip[...].astype(F32)
+    s.pack[pl.ds(at.bias, 1), :] = s.conv_b[...].astype(F32)[None, :]
+    s.pack[pl.ds(at.dt_bias, 1), :] = s.dt_bias[...].astype(F32)[None, :]
+    s.pack[pl.ds(at.skip, 1), :] = s.d_skip[...].astype(F32)[None, :]
     s.pack[pl.ds(at.gain, 1), :] = jnp.zeros((1, EH), F32)
-    s.pack[pl.ds(at.gain, 1), pl.ds(0, DH)] = s.gain_own[...].astype(F32)
+    s.pack[pl.ds(at.gain, 1), pl.ds(0, DH)] = s.gain_own[...].astype(F32)[None, :]
     pl.semaphore_wait(barrier, LEVELS + 1)
 
     width = 2 * E // 6
@@ -568,7 +592,7 @@
     for j in range(6):
         cols = pl.ds(j * width, width)
         gathers.append(remote(s.w_in_own.at[:, cols], s.w_in.at[mine_d, cols], 1 + j, peer))
-    gathers.append(remote(s.w_x_own, s.w_x.at[mine_e, :], 7, peer))
+    gathers.append(remote(s.w_xt_own, s.w_xt_in, 7, peer))
     gathers.append(remote(s.w_dt_own, s.w_dt_in, 8, peer))
     gathers.append(remote(s.w_out_own, s.w_out.at[mine_e, :], 9, peer))
     for copy in gathers:
@@ -585,7 +609,7 @@
 
     start_norm(s)
     swaps[1].start()
-    s.w_x[mine_e, :] = s.w_x_own[...]
+    s.w_xt[:, mine_e] = s.w_xt_own[...]
     s.w_dt[:, mine_e] = s.w_dt_own[...]
     s.small[:, mine_e] = s.pack[...]
     s.gain[:, mine_d] = s.pack[pl.ds(at.gain, 1), pl.ds(0, DH)]
@@ -602,6 +626,7 @@
     gathers[7].wait_recv()
     gathers[8].wait_recv()
     s.w_dt[:, theirs_e] = s.w_dt_in[...]
+    s.w_xt[:, theirs_e] = s.w_xt_in[...]
     scan_inputs(s)
     for j in range(3):
         gathers[4 + j].wait_recv()
@@ -646,35 +671,31 @@
         grad_in(1, color, s.d_gate, s.d_gate_in)
         units[3 + color].start()
 
-    def event(unit, step):
-        members = units[9:] if unit == 3 else units[3 * unit : 3 * unit + 3]
-        for member in members:
+    def carry_on(events):
+        for index, step in events:
             if step < LEVELS:
-                member.reduce(step)
+                units[index].reduce(step)
             else:
-                member.spread(2 * LEVELS - 1 - step)
-
-    schedule = {6: (0, 0), 10: (1, 0), 12: (0, 1), 14: (1, 1), 15: (0, 2)}
+                units[index].spread(2 * LEVELS - 1 - step)
 
     def between(k):
-        for when, what in schedule.items():
-            pl.when(k == when)(functools.partial(event, *what))
+        for when, events in DURING.items():
+            if when < s.T // STEPS:
+                pl.when(k == when)(functools.partial(carry_on, events))
+
+    def phase(number, step):
+        step(s)
+        carry_on(DURING.get(number, ()))
 
     s.rows[pl.ds(at.gain, 1), :] = jnp.zeros((1, E), F32)
     backward_scan(s, between)
-    event(1, 2)
-    back_step(s)
-    event(0, 3)
-    back_proj(s)
-    event(1, 3)
+    phase(16, back_step)
+    phase(17, back_proj)
     back_conv(s)
     swaps[4].start()
-    event(0, 4)
-    event(1, 4)
-    back_in(s)
-    event(0, 5)
-    event(1, 5)
-    back_norm(s)
+    carry_on(DURING.get(18, ()))
+    phase(19, back_in)
+    phase(20, back_norm)
     s.rows[pl.ds(at.gain, 1), pl.ds(0, DH)] = s.d_gain[:, pl.ds(0, DH)]
     s.rows[pl.ds(at.gain, 1), pl.ds(EH, DH)] = s.d_gain[:, pl.ds(DH, DH)]
     swaps[5].start()
@@ -691,34 +712,26 @@
         value = jnp.concatenate([value, jnp.zeros((160 - total, 256), F32)], axis=0)
         s.acc_rows[pl.ds(160 * part, 160), :] = value.astype(BF16)
     units[9].start()
-    event(0, 6)
-    event(1, 6)
-    event(2, 0)
-    event(3, 0)
-    event(0, 7)
-    event(1, 7)
-    for step in range(1, 2 * LEVELS):
-        event(2, step)
-        event(3, step)
+    carry_on(AFTER)
     for copy in gathers + swaps:
         copy.wait_send()
     for unit in units:
         unit.finish()
 
 
-def fused_layer(length, tokens, cotangent, gain, w_in, conv_w, conv_b, w_x, w_dt, dt_bias, a_log, d_skip, w_out):
-    z = sizes(tokens, jax.ShapeDtypeStruct((2 * w_out.shape[0], w_out.shape[1]), BF16), a_log, w_dt, w_x, conv_w)
+def fused_layer(length, tokens, cotangent, gain, w_in, conv_w, conv_b, w_xt, w_dt, dt_bias, a_log, d_skip, w_out):
+    z = sizes(tokens, jax.ShapeDtypeStruct((2 * w_out.shape[0], w_out.shape[1]), BF16), a_log, w_dt, w_xt, conv_w)
     T, D, E, N, R, J, K = (z[n] for n in "TDENRJK")
     DH, EH = D // 2, E // 2
     total = N + K + 4 + R + J
-    names = ("length", "tok", "cot", "gain_own", "w_in_own", "conv_w", "conv_b", "w_x_own", "w_dt_own", "dt_bias", "a_log", "d_skip", "w_out_own")
+    names = ("length", "tok", "cot", "gain_own", "w_in_own", "conv_w", "conv_b", "w_xt_own", "w_dt_own", "dt_bias", "a_log", "d_skip", "w_out_own")
     outs = dict(
         output=((T, D), BF16), input_grad=((T, D), F32), out=((9 * 256, D), BF16), out_rows=((512, 256), BF16)
     )
     plan = scratch_plan(z)
     plan.update(
-        w_in=((D, 2 * E), BF16), w_out=((E, D), BF16), w_x=((E, J), BF16), w_dt=((R, E), BF16),
-        pack=((N + K + 4, EH), F32), pack_in=((N + K + 4, EH), F32), w_dt_in=((R, EH), BF16),
+        w_in=((D, 2 * E), BF16), w_out=((E, D), BF16), w_xt=((J, E), BF16), w_dt=((R, E), BF16),
+        pack=((N + K + 4, EH), F32), pack_in=((N + K + 4, EH), F32), w_dt_in=((R, EH), BF16), w_xt_in=((J, EH), BF16),
         normed=((T, D), BF16), gated=((T, E), BF16), d_branch=((T, D), BF16), d_inner=((T, E), BF16),
         d_gate=((T, E), BF16), rows=((total, E), F32), normed_in=((T, DH), BF16), d_branch_in=((T, D), BF16),
         gated_in=((T, EH), BF16), d_gate_in=((T, E), BF16), d_inner_in=((T, E), BF16), rows_in=((total, EH), F32),
@@ -737,53 +750,85 @@
         + [pltpu.SemaphoreType.DMA((2,)), pltpu.SemaphoreType.DMA((sems,)), pltpu.SemaphoreType.DMA((sems,))],
         compiler_params=pltpu.CompilerParams(collective_id=0, has_side_effects=True, vmem_limit_bytes=63 * MB),
         name="layer",
-    )(length, tokens, cotangent, gain, w_in, conv_w, conv_b, w_x, w_dt, dt_bias, a_log, d_skip, w_out)
-
-
-def finish_kernel(N, K, R, J, out, out_rows, output_in, grad_in_in, output, input_grad, *grads):
-    g_gain, g_in, g_conv_w, g_conv_b, g_x, g_dt, g_dt_bias, g_a_log, g_skip, g_out = grads
-    output[...] = output_in[...]
-    input_grad[...] = grad_in_in[...]
+    )(length, tokens, cotangent, gain, w_in, conv_w, conv_b, w_xt, w_dt, dt_bias, a_log, d_skip, w_out)
+
+
+def finish_kernel(N, K, R, J, *refs):
+    out, out_rows, output_in, input_grad_in, output, input_grad = refs[:6]
+    g_gain, g_in, g_conv_w, g_conv_b, g_xt, g_dt, g_dt_bias, g_a_log, g_skip, g_out = refs[6:16]
+    low, wide, kept, kept_wide, sem_in, sem_out = refs[16:]
     DH, D = g_in.shape[0], out.shape[1]
-    g_out[...] = out[pl.ds(0, D), :].astype(F32)
-    for place, unit in enumerate((2, 1)):
-        for half in range(2):
-            g_in[:, pl.ds((2 * place + half) * D, D)] = out[pl.ds(unit * D + half * DH, DH), :].astype(F32)
+    size = 128
+    count = out.shape[0] // size
+    reads, writes = [], []
+    for index in range(count):
+        rows = pl.ds(index * size, size)
+        reads.append(pltpu.make_async_copy(out.at[rows, :], low.at[rows, :], sem_in.at[index]))
+        unit, first = index * size // D, index * size % D
+        if unit == 0:
+            target = g_out.at[pl.ds(first, size), :]
+        else:
+            place = (2 - unit) * 2 + first // DH
+            target = g_in.at[pl.ds(first % DH, size), pl.ds(place * D, D)]
+        writes.append(pltpu.make_async_copy(wide.at[rows, :], target, sem_out.at[index]))
+    for index, (source, held, target) in enumerate(
+        ((input_grad_in, kept_wide, input_grad), (output_in, kept, output))
+    ):
+        reads.append(pltpu.make_async_copy(source, held, sem_in.at[count + index]))
+        writes.append(pltpu.make_async_copy(held, target, sem_out.at[count + index]))
+    for copy in reads:
+        copy.start()
     M = N + K + 4
     for part in range(3):
         value = out_rows[pl.ds(160 * part, 160), :].astype(F32)
         cols = pl.ds(256 * part, 256)
         g_a_log[:, cols] = value[:N]
         g_conv_w[:, cols] = value[N : N + K]
-        g_conv_b[:, cols] = value[N + K : N + K + 1]
-        g_dt_bias[:, cols] = value[N + K + 1 : N + K + 2]
-        g_skip[:, cols] = value[N + K + 2 : N + K + 3]
-        row = value[N + K + 3 : N + K + 4]
+        g_conv_b[cols] = value[N + K]
+        g_dt_bias[cols] = value[N + K + 1]
+        g_skip[cols] = value[N + K + 2]
         if part == 0:
-            g_gain[:, pl.ds(0, 256)] = row
+            g_gain[pl.ds(0, 256)] = value[N + K + 3]
         elif part == 1:
-            g_gain[:, pl.ds(256, DH - 256)] = row[:, : DH - 256]
+            g_gain[pl.ds(256, DH - 256)] = value[N + K + 3, : DH - 256]
         g_dt[:, cols] = value[M : M + R]
-        turned = jnp.concatenate([value[M + R : M + R + J], jnp.zeros((128 - J, 256), F32)], axis=0).T
-        g_x[cols, :] = turned[:, :J]
+        g_xt[:, cols] = value[M + R : M + R + J]
+    for index in range(count):
+        rows = pl.ds(index * size, size)
+        reads[index].wait()
+        wide[rows, :] = low[rows, :].astype(F32)
+        writes[index].start()
+    for index in range(count, count + 2):
+        reads[index].wait()
+        writes[index].start()
+    for copy in writes:
+        copy.wait()
 
 
 def fused_body(tokens, lengths, cotangent, *shards):
-    shards = [w.reshape(1, -1) if w.ndim == 1 else w for w in shards]
+    shards = list(shards)
+    shards[4] = shards[4].T
     output, input_grad, out, out_rows = fused_layer(lengths, tokens[0], cotangent[0], *shards)
-    gain, w_in, conv_w, conv_b, w_x, w_dt, dt_bias, a_log, d_skip, w_out = shards
+    gain, w_in, conv_w, conv_b, w_xt, w_dt, dt_bias, a_log, d_skip, w_out = shards
+    chunks = out.shape[0] // 128
+    specs = [VMEM] * 12
+    specs[0] = specs[1] = specs[3] = specs[11] = ANY
     results = pl.pallas_call(
-        functools.partial(finish_kernel, a_log.shape[0], conv_w.shape[0], w_dt.shape[0], w_x.shape[1]),
+        functools.partial(finish_kernel, a_log.shape[0], conv_w.shape[0], w_dt.shape[0], w_xt.shape[0]),
         out_shape=[jax.ShapeDtypeStruct(x.shape, x.dtype) for x in (output, input_grad)]
         + [jax.ShapeDtypeStruct(w.shape, F32) for w in shards],
-        in_specs=[VMEM] * 4,
-        out_specs=[VMEM] * 12,
+        in_specs=[ANY, VMEM, ANY, ANY],
+        out_specs=specs,
+        scratch_shapes=[
+            pltpu.VMEM(out.shape, BF16), pltpu.VMEM(out.shape, F32), pltpu.VMEM(output.shape, BF16),
+            pltpu.VMEM(output.shape, F32), pltpu.SemaphoreType.DMA((chunks + 2,)),
+            pltpu.SemaphoreType.DMA((chunks + 2,)),
+        ],
         compiler_params=pltpu.CompilerParams(vmem_limit_bytes=60 * MB),
         name="finish",
     )(out, out_rows, output, input_grad)
     output, input_grad, *grads = results
-    vectors = (0, 3, 6, 8)
-    grads = [g.reshape(-1) if i in vectors else g for i, g in enumerate(grads)]
+    grads[4] = grads[4].T
     return (output[None], input_grad[None], *grads)
 
 

time: 151 us -> 115 us (0.76)
  Pallas kernels: 135 us -> 113 us
  local copies, waits for them, and re-layouts: 8.59 us -> 0 us
  other arithmetic: 5.12 us -> 0 us
    pallas_call x1, Pallas kernels: 129 us -> 106 us  [fused_layer(): pl.pallas_call(functools.partial(fused_kernel, z, names), out_shape=[jax....]
    pallas_call x4 -> x0, other arithmetic: 5.12 us -> none  [fused_body(): pl.pallas_call(functools.partial(finish_kernel, a_log.shape[0], conv_w.sh...]
    reshape x4 -> x0, local copies, waits for them, and re-layouts: 5.03 us -> none  [fused_body(): shards = [w.reshape(1, -1) if w.ndim == 1 else w for w in shards]]
    unnamed x2 -> x0, local copies, waits for them, and re-layouts: 3.56 us -> none
where the time goes in v3:
time: 115 us; the launch traced here: 114 us
  Pallas kernels  113 us (98%)
  between operations  1.3 us (1%)
    pallas_call x1, Pallas kernels, fused_layer(): pl.pallas_call(functools.partial(fused_kernel, z, names), out_shape=[jax....  106 us
    pallas_call x1, Pallas kernels, fused_body(): pl.pallas_call(functools.partial(finish_kernel, a_log.shape[0], conv_w.sh...  6.61 us

profile of v3, /device:TPU:0, one launch (start us, length us, event | category | flops | bytes accessed | tf_op | source)
XLA Modules:
  0.0 114.3 jit_solution(16392281766739470872)
XLA Ops:
  1.3 106.4 %layer.1 = (bf16[256,768]{1,0:T(8,128)(2,1)}, f32[256,768]{1,0:T(8,128)}, bf16[2304,768]{1,0:T(8,128)(2,1)}, bf16[512,256]{1,0:T(8,128)(2,1)}) custom-call(s32[1]{0:T(128)S(6)} %copy.25.refs_0_, bf16[256,768]{1,0:T(8,128)(2,1)} %bitcast.6, bf16[256,768]{1,0:T(8,128)(2,1)} %bitcast.7, bf16[384]{0:T(512)(128)(2,1)} %refs_3_.1, bf16[384,3072]{1,0:T(8,128)(2,1)} %refs_4_.1, ...), custom_call_target="tpu_custom_call" | custom-call | tf_op jit(solution)/shard_map/layer/pallas_call | solution.py:744
  107.7 6.6 %finish.1 = (bf16[256,768]{1,0:T(8,128)(2,1)}, f32[256,768]{1,0:T(8,128)}, f32[384]{0:T(512)}, f32[384,3072]{1,0:T(8,128)}, f32[4,768]{1,0:T(4,128)}, /*index=5*...) custom-call(bf16[2304,768]{1,0:T(8,128)(2,1)} %get-tuple-element.28., ...), custom_call_target="tpu_custom_call" | custom-call | tf_op jit(solution)/shard_map/finish/pallas_call | solution.py:816

commit v4 on v3

--- a/solution.py
+++ b/solution.py
@@ -31,12 +31,12 @@
     return pl.ds(pl.multiple_of(index * size, size), size)
 
 
-def repeat(count, step):
+def repeat(count, step, unroll=1):
     def run(index, carry):
         step(index)
         return carry
 
-    lax.fori_loop(0, count, run, 0)
+    lax.fori_loop(0, count, run, 0, unroll=min(unroll, count))
 
 
 def row_plan(s):
@@ -54,7 +54,7 @@
         live = (at < s.length[0]).astype(F32)
         s.d_branch[rows, :] = (live * s.cot[rows, :].astype(F32)).astype(BF16)
 
-    repeat(s.T // 64, run)
+    repeat(s.T // 64, run, 4)
 
 
 def norm(s):
@@ -63,7 +63,7 @@
         x = s.tok[rows, :].astype(F32)
         s.normed[rows, :] = (x * s.inv[rows, pl.ds(0, 1)] * s.gain[...]).astype(BF16)
 
-    repeat(s.T // 64, run)
+    repeat(s.T // 64, run, 4)
 
 
 def project_inner(s, first, count):
@@ -73,7 +73,7 @@
         cols = span(first + index, 256)
         s.inner[pl.ds(PAD, s.T), cols] = dot(s.normed[...], s.w_in[:, cols])
 
-    repeat(count, run)
+    repeat(count, run, 6)
 
     def convolve(index):
         cols = span(2 * first + index, 128)
@@ -85,7 +85,7 @@
         s.active[:, cols] = (value * sigma).astype(BF16)
         s.cslope[:, cols] = sigma * (1.0 + value * (1.0 - sigma))
 
-    repeat(2 * count, convolve)
+    repeat(2 * count, convolve, 4)
 
 
 def project_gate(s, first, count):
@@ -97,7 +97,7 @@
         s.gact[:, cols] = value * sigma
         s.gslope[:, cols] = sigma * (1.0 + value * (1.0 - sigma))
 
-    repeat(count, run)
+    repeat(count, run, 6)
 
 
 def diagonal(s):
@@ -123,7 +123,7 @@
         parts = [(jnp.broadcast_to(rows[i : i + 1], (N, J)) * mask).astype(BF16) for i in range(STEPS)]
         s.spread[span(block, wide), :] = dot(jnp.concatenate(parts, axis=0), ones)
 
-    repeat(s.T // STEPS, run)
+    repeat(s.T // STEPS, run, 4)
 
 
 def scan_inputs(s):
@@ -146,7 +146,7 @@
         s.step[:, cols] = size
         s.sigp[:, cols] = jax.nn.sigmoid(pre)
 
-    repeat(s.E // 256, run)
+    repeat(s.E // 256, run, 6)
     s.decay[...] = -jnp.exp(s.small[pl.ds(0, s.N), :]) * LOG2E
 
 
@@ -186,7 +186,7 @@
         s.mixed[pl.ds(0, s.T), cols] = value
         s.gated[:, cols] = (value * s.gact[:, cols]).astype(BF16)
 
-    repeat(s.E // 128, run)
+    repeat(s.E // 128, run, 2)
 
 
 def back_out(s):
@@ -202,7 +202,7 @@
             d_value * s.active[:, cols].astype(F32), axis=0, keepdims=True
         )
 
-    repeat(s.E // 256, run)
+    repeat(s.E // 256, run, 6)
 
 
 def project_out(s):
@@ -213,7 +213,7 @@
         live = (at < s.length[0]).astype(F32)
         s.output[:, cols] = (s.tok[:, cols].astype(F32) + live * branch).astype(BF16)
 
-    repeat(s.D // 256, run)
+    repeat(s.D // 256, run, 3)
 
 
 def backward_scan(s, between=None):
@@ -299,13 +299,13 @@
     s.d_proj[:, pl.ds(s.R + s.N, s.N)] = dot((s.dc[...] * mask).astype(BF16), pick).astype(BF16)
 
 
-def back_conv(s):
+def back_conv(s, part, count):
     at = row_plan(s)
     s.mixed[pl.ds(s.T, PAD), :] = jnp.zeros((PAD, s.E), F32)
     first = at.gain + 1
 
     def run(index):
-        cols = span(index, 128)
+        cols = span(part + index, 128)
         s.rows[pl.ds(first, s.R), cols] = dot(s.proj[:, : s.R], s.d_pre_low[:, cols], (0, 0))
         s.rows[pl.ds(first + s.R, s.J), cols] = dot(s.d_proj[...], s.active[:, cols], (0, 0))
         d_active = s.d_mixed[:, cols] + dot(s.d_proj[...], s.w_xt[:, cols])
@@ -321,7 +321,7 @@
             total = total + taps * s.mixed[pl.ds(s.K - 1 - k, s.T), cols]
         s.d_inner[:, cols] = total.astype(BF16)
 
-    repeat(s.E // 128, run)
+    repeat(count, run, 6)
 
 
 def back_in(s):
@@ -331,7 +331,7 @@
             s.d_gate[...], s.w_in[rows, pl.ds(s.E, s.E)], (1, 1)
         )
 
-    repeat(s.D // 256, run)
+    repeat(s.D // 256, run, 3)
 
 
 def back_norm(s):
@@ -349,7 +349,7 @@
             s.cot[rows, :].astype(F32) + scale * d_scaled - x * (scale * scale * scale) * shared
         )
 
-    repeat(s.T // 64, run)
+    repeat(s.T // 64, run, 4)
 
 
 def sizes(tokens, w_out, a_log, w_dt, w_xt, conv_w):
@@ -393,8 +393,11 @@
     for step in (scan_inputs, forward_scan, mix, project_out, back_out):
         step(s)
     backward_scan(s)
-    for step in (back_step, back_proj, back_conv, back_in, back_norm):
-        step(s)
+    back_step(s)
+    back_proj(s)
+    back_conv(s, 0, s.E // 128)
+    back_in(s)
+    back_norm(s)
     s.g_gain[...] = s.d_gain[...]
 
 
@@ -448,24 +451,42 @@
 
 
 ORDERS = (
-    (0, 1, 2, 3), (1, 0, 3, 2), (3, 1, 0, 2), (0, 1, 2, 3), (1, 0, 3, 2),
-    (2, 0, 1, 3), (1, 0, 3, 2), (2, 0, 1, 3), (0, 1, 2, 3), (1, 0, 2, 3),
+    ((3,), (0,), (1,), (2,)),
+    ((2,), (1,), (0,), (3,)),
+    ((0,), (2,), (1,), (3,)),
+    ((0, 1), (2, 3)),
+    ((0,), (1,), (2,), (3,)),
+    ((1,), (0,), (2,), (3,)),
+    ((1,), (0,), (2, 3)),
+    ((0,), (1,), (2, 3)),
+    ((2,), (0, 1), (3,)),
+    ((1,), (0,), (2, 3)),
 )
 DURING = {
-    5: ((0, 0), (1, 0)), 10: ((3, 0), (4, 0), (2, 0), (5, 0)), 12: ((1, 1),), 13: ((0, 1),),
-    15: ((4, 1), (3, 1)), 17: ((1, 2), (0, 2)), 18: ((5, 1), (2, 1), (3, 2), (4, 2)), 19: ((1, 3), (0, 3)),
+    6: ((2, 0),),
+    9: ((0, 0), (1, 0), (3, 0)),
+    11: ((2, 1), (5, 0)),
+    13: ((3, 1), (4, 0), (1, 1)),
+    14: ((2, 2),),
+    15: ((0, 1),),
+    17: ((5, 1), (4, 1), (3, 2)),
+    18: ((2, 3), (1, 2), (0, 2)),
+    19: ((5, 2),),
+    20: ((4, 2),),
+    21: ((2, 4),),
+    22: ((1, 3), (0, 3), (3, 3)),
 }
 AFTER = (
-    (5, 2), (2, 2), (3, 3), (4, 3), (1, 4), (0, 4), (6, 0), (8, 0), (7, 0), (5, 3), (2, 3), (3, 4), (4, 4), (9, 0),
-    (6, 1), (0, 5), (1, 5), (8, 1), (7, 1), (5, 4), (2, 4), (3, 5), (9, 1), (0, 6), (4, 5), (1, 6), (7, 2), (2, 5),
-    (5, 5), (6, 2), (8, 2), (9, 2), (3, 6), (7, 3), (6, 3), (8, 3), (0, 7), (9, 3), (6, 4), (7, 4), (4, 6), (1, 7),
-    (8, 4), (9, 4), (5, 6), (2, 6), (6, 5), (8, 5), (7, 5), (9, 5), (3, 7), (4, 7), (5, 7), (6, 6), (8, 6), (7, 6),
-    (9, 6), (6, 7), (8, 7), (2, 7), (7, 7), (9, 7),
+    (5, 3), (6, 0), (7, 0), (8, 0), (2, 5), (4, 3), (0, 4), (1, 4), (5, 4), (6, 1), (9, 0), (2, 6),
+    (7, 1), (4, 4), (5, 5), (1, 5), (8, 1), (9, 1), (6, 2), (0, 5), (7, 2), (4, 5), (1, 6), (8, 2),
+    (2, 7), (9, 2), (4, 6), (5, 6), (6, 3), (0, 6), (7, 3), (1, 7), (5, 7), (8, 3), (4, 7), (9, 3),
+    (7, 4), (6, 4), (8, 4), (9, 4), (6, 5), (0, 7), (7, 5), (8, 5), (9, 5),
 )
-LEVELS = 4
-PIECES = 2**LEVELS
+PIECES = 16
+FIRST, SECOND = 0, 2
 GATHERS = 10
-SWAPS = 6
+SWAPS = 7
+COPIES = 12
 
 
 def packed_rows(s):
@@ -473,72 +494,91 @@
 
 
 class Sum:
-    def __init__(self, s, sem, order, acc, recv, out, first, piece):
-        self.s, self.sem, self.order, self.piece = s, sem, order, piece
+    def __init__(self, s, number, stages, acc, recv, out, result, first, piece):
+        self.s, self.stages, self.piece, self.steps = s, stages, piece, 2 * len(stages)
+        self.sem = GATHERS + SWAPS + COPIES * number
         self.acc, self.recv, self.out = acc, recv, out
-        self.first, self.first_recv = first * PIECES * piece, first * (PIECES - 1) * piece
-        self.bit = [lax.rem(s.dp // 2**b, 2) for b in order]
-
-    def partner(self, level):
-        b = self.order[level]
-        return (self.s.dp + (1 - 2 * self.bit[level]) * 2**b, self.s.me)
-
-    def rows(self, level, mine):
-        start = 0
-        for above in range(level):
-            start = start + self.bit[above] * (PIECES >> (above + 1))
-        bit = self.bit[level] if mine else 1 - self.bit[level]
-        start = start + bit * (PIECES >> (level + 1))
-        count = (PIECES >> (level + 1)) * self.piece
-        return pl.multiple_of(self.first + start * self.piece, 16), count
-
-    def landing(self, level):
-        start = self.first_recv + (PIECES - (PIECES >> level)) * self.piece
-        return start, (PIECES >> (level + 1)) * self.piece
-
-    def reduce_copy(self, level):
-        return self.s.remote(
-            self.acc.at[pl.ds(*self.rows(level, False)), :],
-            self.recv.at[pl.ds(*self.landing(level)), :],
-            self.sem + level, self.partner(level),
-        )
-
-    def spread_copy(self, level, mine=True):
-        rows = pl.ds(*self.rows(level, mine))
-        return self.s.remote(
-            self.out.at[rows, :], self.out.at[rows, :], self.sem + LEVELS + level, self.partner(level)
-        )
+        self.first, self.landed = first * PIECES * piece, first * (PIECES - 1) * piece
+        self.bits = [[lax.rem(s.dp // 2**b, 2) for b in stage] for stage in stages]
+        whole = pl.ds(self.first, PIECES * piece)
+        self.leave = pltpu.make_async_copy(out.at[whole, :], result.at[whole, :], s.local.at[6 + number])
+        self.plan = []
+        start, count, landing, sem = 0, PIECES, 0, self.sem
+        for stage, bits in zip(stages, self.bits):
+            group = 2 ** len(stage)
+            count //= group
+            others = []
+            for flip in range(1, group):
+                device, place = s.dp, 0
+                for j, (b, bit) in enumerate(zip(stage, bits)):
+                    flipped = flip // 2**j % 2
+                    device = device + flipped * (1 - 2 * bit) * 2**b
+                    place = place + (flipped + (1 - 2 * flipped) * bit) * 2**j
+                others.append(((device, s.me), start + place * count, landing, sem))
+                landing, sem = landing + count, sem + 2
+            for j, bit in enumerate(bits):
+                start = start + bit * 2**j * count
+            self.plan.append((others, start, count))
+
+    def rows(self, start, count):
+        return pl.ds(pl.multiple_of(self.first + start * self.piece, 16), count * self.piece)
+
+    def reduce_copies(self, level):
+        others, _, count = self.plan[level]
+        return [
+            self.s.remote(
+                self.acc.at[self.rows(theirs, count), :],
+                self.recv.at[pl.ds(self.landed + landing * self.piece, count * self.piece), :], sem, device,
+            )
+            for device, theirs, landing, sem in others
+        ]
+
+    def spread_copies(self, level, sent=True):
+        others, mine, count = self.plan[level]
+        copies = []
+        for device, theirs, _, sem in others:
+            rows = self.rows(mine if sent else theirs, count)
+            copies.append(self.s.remote(self.out.at[rows, :], self.out.at[rows, :], sem + 1, device))
+        return copies
 
     def start(self):
-        self.reduce_copy(0).start()
+        for copy in self.reduce_copies(0):
+            copy.start()
+
+    def carry_on(self, step):
+        levels = len(self.stages)
+        if step < levels:
+            self.reduce(step)
+            following = self.spread_copies(step) if step == levels - 1 else self.reduce_copies(step + 1)
+        else:
+            level = self.steps - 1 - step
+            for copy in self.spread_copies(level, False):
+                copy.wait_recv()
+            following = self.spread_copies(level - 1) if level > 0 else [self.leave]
+        for copy in following:
+            copy.start()
 
     def reduce(self, level):
-        self.reduce_copy(level).wait_recv()
-        start, count = self.rows(level, True)
-        landed = self.landing(level)[0]
-        last = level == LEVELS - 1
-        target = self.out if last else self.acc
+        for copy in self.reduce_copies(level):
+            copy.wait_recv()
+        others, mine, count = self.plan[level]
+        target = self.out if level == len(self.stages) - 1 else self.acc
 
         def add(index):
-            here = pl.ds(pl.multiple_of(start + index * self.piece, 16), self.piece)
-            there = pl.ds(pl.multiple_of(landed + index * self.piece, 16), self.piece)
-            target[here, :] = (self.acc[here, :].astype(F32) + self.recv[there, :].astype(F32)).astype(BF16)
-
-        repeat(count // self.piece, add)
-        if last:
-            self.spread_copy(level).start()
-        else:
-            self.reduce_copy(level + 1).start()
-
-    def spread(self, level):
-        self.spread_copy(level, False).wait_recv()
-        if level > 0:
-            self.spread_copy(level - 1).start()
+            here = self.rows(mine + index, 1)
+            total = self.acc[here, :].astype(F32)
+            for _, _, landing, _ in others:
+                there = pl.ds(pl.multiple_of(self.landed + (landing + index) * self.piece, 16), self.piece)
+                total = total + self.recv[there, :].astype(F32)
+            target[here, :] = total.astype(BF16)
+
+        repeat(count, add)
 
     def finish(self):
-        for level in range(LEVELS):
-            self.reduce_copy(level).wait_send()
-            self.spread_copy(level).wait_send()
+        for level in range(len(self.stages)):
+            for copy in self.reduce_copies(level) + self.spread_copies(level):
+                copy.wait_send()
+        self.leave.wait()
 
 
 def fused_kernel(z, names, *refs):
@@ -558,26 +598,30 @@
         )
 
     s.remote = remote
-    units = []
-    for unit in range(3):
-        for color in range(3):
-            index = 3 * unit + color
-            units.append(
-                Sum(s, GATHERS + SWAPS + 2 * LEVELS * index, ORDERS[index], s.acc, s.recv, s.out, index, 16)
-            )
-    units.append(Sum(s, GATHERS + SWAPS + 2 * LEVELS * 9, ORDERS[9], s.acc_rows, s.recv_rows, s.out_rows, 0, 32))
+    units = [Sum(s, i, ORDERS[i], s.acc, s.recv, s.out, s.out_to, i, 16) for i in range(9)]
+    units.append(Sum(s, 9, ORDERS[9], s.acc_rows, s.recv_rows, s.out_rows, s.out_rows_to, 0, 32))
 
     barrier = pltpu.get_barrier_semaphore()
     pl.semaphore_signal(barrier, inc=1, device_id=peer, device_id_type=MESH)
-    for level in range(LEVELS):
-        pl.semaphore_signal(barrier, inc=1, device_id=units[0].partner(level), device_id_type=MESH)
+    partners = {}
+    for unit in units:
+        for stage, (others, _, _) in zip(unit.stages, unit.plan):
+            for flip, other_one in enumerate(others):
+                partners[(stage, flip)] = other_one[0]
+    greeted = {}
+    for (stage, flip), device in partners.items():
+        greeted[tuple(sorted(b for j, b in enumerate(stage) if (flip + 1) // 2**j % 2))] = device
+    for device in greeted.values():
+        pl.semaphore_signal(barrier, inc=1, device_id=device, device_id_type=MESH)
 
     mine_d, mine_e = span(s.me, DH), span(s.me, EH)
     theirs_d, theirs_e = span(other, DH), span(other, EH)
     local_in = pltpu.make_async_copy(s.w_in_own, s.w_in.at[mine_d, :], s.local.at[0])
     local_out = pltpu.make_async_copy(s.w_out_own, s.w_out.at[mine_e, :], s.local.at[1])
-    local_in.start()
-    local_out.start()
+    local_tok = pltpu.make_async_copy(s.tok_own, s.tok, s.local.at[2])
+    local_cot = pltpu.make_async_copy(s.cot_own, s.cot, s.local.at[3])
+    for copy in (local_tok, local_cot, local_in, local_out):
+        copy.start()
     s.pack[pl.ds(0, s.N), :] = s.a_log[...].astype(F32)
     s.pack[pl.ds(at.conv, s.K), :] = s.conv_w[...].astype(F32)
     s.pack[pl.ds(at.bias, 1), :] = s.conv_b[...].astype(F32)[None, :]
@@ -585,7 +629,7 @@
     s.pack[pl.ds(at.skip, 1), :] = s.d_skip[...].astype(F32)[None, :]
     s.pack[pl.ds(at.gain, 1), :] = jnp.zeros((1, EH), F32)
     s.pack[pl.ds(at.gain, 1), pl.ds(0, DH)] = s.gain_own[...].astype(F32)[None, :]
-    pl.semaphore_wait(barrier, LEVELS + 1)
+    pl.semaphore_wait(barrier, len(greeted) + 1)
 
     width = 2 * E // 6
     gathers = [remote(s.pack, s.pack_in, 0, peer)]
@@ -595,18 +639,21 @@
     gathers.append(remote(s.w_xt_own, s.w_xt_in, 7, peer))
     gathers.append(remote(s.w_dt_own, s.w_dt_in, 8, peer))
     gathers.append(remote(s.w_out_own, s.w_out.at[mine_e, :], 9, peer))
-    for copy in gathers:
-        copy.start()
+    for j in (0, 1, 2, 3, 7, 8, 4, 5, 6, 9):
+        gathers[j].start()
 
     swaps = [
         remote(s.normed.at[:, theirs_d], s.normed_in, GATHERS, peer),
         remote(s.d_branch, s.d_branch_in, GATHERS + 1, peer),
         remote(s.gated.at[:, theirs_e], s.gated_in, GATHERS + 2, peer),
         remote(s.d_gate, s.d_gate_in, GATHERS + 3, peer),
-        remote(s.d_inner, s.d_inner_in, GATHERS + 4, peer),
-        remote(s.rows.at[:, theirs_e], s.rows_in, GATHERS + 5, peer),
+        remote(s.d_inner.at[:, pl.ds(0, EH)], s.d_inner_in.at[:, pl.ds(0, EH)], GATHERS + 4, peer),
+        remote(s.d_inner.at[:, pl.ds(EH, EH)], s.d_inner_in.at[:, pl.ds(EH, EH)], GATHERS + 5, peer),
+        remote(s.rows.at[:, theirs_e], s.rows_in, GATHERS + 6, peer),
     ]
 
+    local_tok.wait()
+    local_cot.wait()
     start_norm(s)
     swaps[1].start()
     s.w_xt[:, mine_e] = s.w_xt_own[...]
@@ -638,8 +685,6 @@
     gathers[9].wait_recv()
     back_out(s)
     swaps[3].start()
-    project_out(s)
-
     def product(left, left_in, right, right_in, shift, cols, across):
         own = pl.ds(pl.multiple_of(shift + cols.start, 128), cols.size)
         total = dot(left[:, own], right[:, across], (0, 0)) + dot(left_in[:, cols], right_in[:, across], (0, 0))
@@ -660,25 +705,27 @@
             )
             first += size
 
-    swaps[1].wait_recv()
-    swaps[2].wait_recv()
-    for color in range(3):
-        grad_out(color)
-        units[color].start()
-    swaps[0].wait_recv()
-    swaps[3].wait_recv()
-    for color in range(3):
-        grad_in(1, color, s.d_gate, s.d_gate_in)
-        units[3 + color].start()
-
     def carry_on(events):
         for index, step in events:
-            if step < LEVELS:
-                units[index].reduce(step)
-            else:
-                units[index].spread(2 * LEVELS - 1 - step)
+            units[index].carry_on(step)
+
+    def first_sums():
+        swaps[1].wait_recv()
+        swaps[2].wait_recv()
+        for color in range(3):
+            grad_out(color)
+            units[color].start()
+
+    def second_sums():
+        swaps[0].wait_recv()
+        swaps[3].wait_recv()
+        for color in range(3):
+            grad_in(1, color, s.d_gate, s.d_gate_in)
+            units[3 + color].start()
 
     def between(k):
+        pl.when(k == FIRST)(first_sums)
+        pl.when(k == SECOND)(second_sums)
         for when, events in DURING.items():
             if when < s.T // STEPS:
                 pl.when(k == when)(functools.partial(carry_on, events))
@@ -691,19 +738,30 @@
     backward_scan(s, between)
     phase(16, back_step)
     phase(17, back_proj)
-    back_conv(s)
+    back_conv(s, 0, 6)
     swaps[4].start()
+    back_conv(s, 6, 6)
+    swaps[5].start()
     carry_on(DURING.get(18, ()))
     phase(19, back_in)
-    phase(20, back_norm)
+    for color in range(3):
+        if color < 2:
+            swaps[4 + color].wait_recv()
+        grad_in(2, color, s.d_inner, s.d_inner_in)
+        units[6 + color].start()
+    carry_on(DURING.get(20, ()))
+    back_norm(s)
     s.rows[pl.ds(at.gain, 1), pl.ds(0, DH)] = s.d_gain[:, pl.ds(0, DH)]
     s.rows[pl.ds(at.gain, 1), pl.ds(EH, DH)] = s.d_gain[:, pl.ds(DH, DH)]
-    swaps[5].start()
-    swaps[4].wait_recv()
-    for color in range(3):
-        grad_in(2, color, s.d_inner, s.d_inner_in)
-        units[6 + color].start()
-    swaps[5].wait_recv()
+    swaps[6].start()
+    leaving = [pltpu.make_async_copy(s.input_grad, s.input_grad_to, s.local.at[5])]
+    leaving[0].start()
+    carry_on(DURING.get(21, ()))
+    project_out(s)
+    leaving.append(pltpu.make_async_copy(s.output, s.output_to, s.local.at[4]))
+    leaving[1].start()
+    carry_on(DURING.get(22, ()))
+    swaps[6].wait_recv()
     total = s.rows.shape[0]
     s.acc_rows[...] = jnp.zeros(s.acc_rows.shape, BF16)
     for part in range(3):
@@ -713,6 +771,8 @@
         s.acc_rows[pl.ds(160 * part, 160), :] = value.astype(BF16)
     units[9].start()
     carry_on(AFTER)
+    for copy in leaving:
+        copy.wait()
     for copy in gathers + swaps:
         copy.wait_send()
     for unit in units:
@@ -724,9 +784,9 @@
     T, D, E, N, R, J, K = (z[n] for n in "TDENRJK")
     DH, EH = D // 2, E // 2
     total = N + K + 4 + R + J
-    names = ("length", "tok", "cot", "gain_own", "w_in_own", "conv_w", "conv_b", "w_xt_own", "w_dt_own", "dt_bias", "a_log", "d_skip", "w_out_own")
+    names = ("length", "tok_own", "cot_own", "gain_own", "w_in_own", "conv_w", "conv_b", "w_xt_own", "w_dt_own", "dt_bias", "a_log", "d_skip", "w_out_own")
     outs = dict(
-        output=((T, D), BF16), input_grad=((T, D), F32), out=((9 * 256, D), BF16), out_rows=((512, 256), BF16)
+        output_to=((T, D), BF16), input_grad_to=((T, D), F32), out_to=((9 * 256, D), BF16), out_rows_to=((512, 256), BF16)
     )
     plan = scratch_plan(z)
     plan.update(
@@ -735,19 +795,21 @@
         normed=((T, D), BF16), gated=((T, E), BF16), d_branch=((T, D), BF16), d_inner=((T, E), BF16),
         d_gate=((T, E), BF16), rows=((total, E), F32), normed_in=((T, DH), BF16), d_branch_in=((T, D), BF16),
         gated_in=((T, EH), BF16), d_gate_in=((T, E), BF16), d_inner_in=((T, E), BF16), rows_in=((total, EH), F32),
+        tok=((T, D), BF16), cot=((T, D), BF16), output=((T, D), BF16), input_grad=((T, D), F32),
+        out=((9 * 256, D), BF16), out_rows=((512, 256), BF16),
         acc=((9 * 256, D), BF16), recv=((9 * 240, D), BF16), acc_rows=((512, 256), BF16), recv_rows=((480, 256), BF16),
     )
-    sems = GATHERS + SWAPS + 2 * LEVELS * 10
+    sems = GATHERS + SWAPS + COPIES * 10
     names = list(names) + list(outs) + list(plan) + ["local", "send", "recv_sem"]
     specs = [SMEM] + [VMEM] * 12
-    specs[4] = specs[12] = ANY
+    specs[1] = specs[2] = specs[4] = specs[12] = ANY
     return pl.pallas_call(
         functools.partial(fused_kernel, z, names),
         out_shape=[jax.ShapeDtypeStruct(*spec) for spec in outs.values()],
         in_specs=specs,
-        out_specs=[VMEM] * len(outs),
+        out_specs=[ANY] * len(outs),
         scratch_shapes=[pltpu.VMEM(*spec) for spec in plan.values()]
-        + [pltpu.SemaphoreType.DMA((2,)), pltpu.SemaphoreType.DMA((sems,)), pltpu.SemaphoreType.DMA((sems,))],
+        + [pltpu.SemaphoreType.DMA((16,)), pltpu.SemaphoreType.DMA((sems,)), pltpu.SemaphoreType.DMA((sems,))],
         compiler_params=pltpu.CompilerParams(collective_id=0, has_side_effects=True, vmem_limit_bytes=63 * MB),
         name="layer",
     )(length, tokens, cotangent, gain, w_in, conv_w, conv_b, w_xt, w_dt, dt_bias, a_log, d_skip, w_out)
@@ -755,32 +817,38 @@
 
 def finish_kernel(N, K, R, J, *refs):
     out, out_rows, output_in, input_grad_in, output, input_grad = refs[:6]
-    g_gain, g_in, g_conv_w, g_conv_b, g_xt, g_dt, g_dt_bias, g_a_log, g_skip, g_out = refs[6:16]
-    low, wide, kept, kept_wide, sem_in, sem_out = refs[16:]
+    targets = refs[6:16]
+    g_in, g_out = targets[1], targets[9]
+    low, wide, rows_low, kept, kept_wide, *small = refs[16:29]
+    sem_in, sem_out = refs[29:]
+    g_gain, g_conv_w, g_conv_b, g_xt, g_dt, g_dt_bias, g_a_log, g_skip = small
     DH, D = g_in.shape[0], out.shape[1]
-    size = 128
-    count = out.shape[0] // size
+    count = out.shape[0] // DH
     reads, writes = [], []
+
+    def through(source, held, held_out, target):
+        index = len(reads)
+        reads.append(pltpu.make_async_copy(source, held, sem_in.at[index]))
+        writes.append(pltpu.make_async_copy(held_out, target, sem_out.at[index]))
+
     for index in range(count):
-        rows = pl.ds(index * size, size)
-        reads.append(pltpu.make_async_copy(out.at[rows, :], low.at[rows, :], sem_in.at[index]))
-        unit, first = index * size // D, index * size % D
+        rows = pl.ds(index * DH, DH)
+        unit, half = index // 2, index % 2
         if unit == 0:
-            target = g_out.at[pl.ds(first, size), :]
+            target = g_out.at[pl.ds(half * DH, DH), :]
         else:
-            place = (2 - unit) * 2 + first // DH
-            target = g_in.at[pl.ds(first % DH, size), pl.ds(place * D, D)]
-        writes.append(pltpu.make_async_copy(wide.at[rows, :], target, sem_out.at[index]))
-    for index, (source, held, target) in enumerate(
-        ((input_grad_in, kept_wide, input_grad), (output_in, kept, output))
-    ):
-        reads.append(pltpu.make_async_copy(source, held, sem_in.at[count + index]))
-        writes.append(pltpu.make_async_copy(held, target, sem_out.at[count + index]))
+            target = g_in.at[:, pl.ds(((2 - unit) * 2 + half) * D, D)]
+        through(out.at[rows, :], low.at[rows, :], wide.at[rows, :], target)
+    through(input_grad_in, kept_wide, kept_wide, input_grad)
+    through(output_in, kept, kept, output)
+    read_rows = pltpu.make_async_copy(out_rows, rows_low, sem_in.at[count + 2])
+    read_rows.start()
     for copy in reads:
         copy.start()
+    read_rows.wait()
     M = N + K + 4
     for part in range(3):
-        value = out_rows[pl.ds(160 * part, 160), :].astype(F32)
+        value = rows_low[pl.ds(160 * part, 160), :].astype(F32)
         cols = pl.ds(256 * part, 256)
         g_a_log[:, cols] = value[:N]
         g_conv_w[:, cols] = value[N : N + K]
@@ -793,13 +861,15 @@
             g_gain[pl.ds(256, DH - 256)] = value[N + K + 3, : DH - 256]
         g_dt[:, cols] = value[M : M + R]
         g_xt[:, cols] = value[M + R : M + R + J]
-    for index in range(count):
-        rows = pl.ds(index * size, size)
+    for index, held in enumerate(small):
+        target = targets[(0, 2, 3, 4, 5, 6, 7, 8)[index]]
+        writes.append(pltpu.make_async_copy(held, target, sem_out.at[count + 2 + index]))
+        writes[-1].start()
+    for index in range(count + 2):
         reads[index].wait()
-        wide[rows, :] = low[rows, :].astype(F32)
-        writes[index].start()
-    for index in range(count, count + 2):
-        reads[index].wait()
+        if index < count:
+            rows = pl.ds(index * DH, DH)
+            wide[rows, :] = low[rows, :].astype(F32)
         writes[index].start()
     for copy in writes:
         copy.wait()
@@ -810,20 +880,16 @@
     shards[4] = shards[4].T
     output, input_grad, out, out_rows = fused_layer(lengths, tokens[0], cotangent[0], *shards)
     gain, w_in, conv_w, conv_b, w_xt, w_dt, dt_bias, a_log, d_skip, w_out = shards
-    chunks = out.shape[0] // 128
-    specs = [VMEM] * 12
-    specs[0] = specs[1] = specs[3] = specs[11] = ANY
+    kept = [out, jax.ShapeDtypeStruct(out.shape, F32), out_rows, output, input_grad]
+    grads = [jax.ShapeDtypeStruct(w.shape, F32) for w in shards]
+    small = [g for i, g in enumerate(grads) if i not in (1, 9)]
     results = pl.pallas_call(
         functools.partial(finish_kernel, a_log.shape[0], conv_w.shape[0], w_dt.shape[0], w_xt.shape[0]),
-        out_shape=[jax.ShapeDtypeStruct(x.shape, x.dtype) for x in (output, input_grad)]
-        + [jax.ShapeDtypeStruct(w.shape, F32) for w in shards],
-        in_specs=[ANY, VMEM, ANY, ANY],
-        out_specs=specs,
-        scratch_shapes=[
-            pltpu.VMEM(out.shape, BF16), pltpu.VMEM(out.shape, F32), pltpu.VMEM(output.shape, BF16),
-            pltpu.VMEM(output.shape, F32), pltpu.SemaphoreType.DMA((chunks + 2,)),
-            pltpu.SemaphoreType.DMA((chunks + 2,)),
-        ],
+        out_shape=[jax.ShapeDtypeStruct(x.shape, x.dtype) for x in (output, input_grad)] + grads,
+        in_specs=[ANY] * 4,
+        out_specs=[ANY] * 12,
+        scratch_shapes=[pltpu.VMEM(x.shape, x.dtype) for x in kept + small]
+        + [pltpu.SemaphoreType.DMA((16,)), pltpu.SemaphoreType.DMA((24,))],
         compiler_params=pltpu.CompilerParams(vmem_limit_bytes=60 * MB),
         name="finish",
     )(out, out_rows, output, input_grad)

time: 115 us -> 102 us (0.89)
  Pallas kernels: 113 us -> 99.8 us
    pallas_call x1, Pallas kernels: 106 us -> 95 us  [fused_layer(): pl.pallas_call(functools.partial(fused_kernel, z, names), out_shape=[jax....]
    pallas_call x1, Pallas kernels: 6.61 us -> 4.84 us  [fused_body(): pl.pallas_call(functools.partial(finish_kernel, a_log.shape[0], conv_w.sh...]
where the time goes in v4:
time: 102 us; the launch traced here: 101 us
  Pallas kernels  99.8 us (98%)
  between operations  1.48 us (1%)
    pallas_call x1, Pallas kernels, fused_layer(): pl.pallas_call(functools.partial(fused_kernel, z, names), out_shape=[jax....  95 us
    pallas_call x1, Pallas kernels, fused_body(): pl.pallas_call(functools.partial(finish_kernel, a_log.shape[0], conv_w.sh...  4.84 us

profile of v4, /device:TPU:0, one launch (start us, length us, event | category | flops | bytes accessed | tf_op | source)
XLA Modules:
  0.0 101.3 jit_solution(7215394750062711090)
XLA Ops:
  1.3 95.0 %layer.1 = (bf16[256,768]{1,0:T(8,128)(2,1)}, f32[256,768]{1,0:T(8,128)}, bf16[2304,768]{1,0:T(8,128)(2,1)}, bf16[512,256]{1,0:T(8,128)(2,1)}) custom-call(s32[1]{0:T(128)S(6)} %copy.25.refs_0_, bf16[256,768]{1,0:T(8,128)(2,1)} %bitcast.6, bf16[256,768]{1,0:T(8,128)(2,1)} %bitcast.7, bf16[384]{0:T(512)(128)(2,1)} %refs_3_.1, bf16[384,3072]{1,0:T(8,128)(2,1)} %refs_4_.1, ...), custom_call_target="tpu_custom_call" | custom-call | tf_op jit(solution)/shard_map/layer/pallas_call | solution.py:806
  96.3 4.8 %finish.1 = (bf16[256,768]{1,0:T(8,128)(2,1)}, f32[256,768]{1,0:T(8,128)}, f32[384]{0:T(512)}, f32[384,3072]{1,0:T(8,128)}, f32[4,768]{1,0:T(4,128)}, /*index=5*...) custom-call(bf16[2304,768]{1,0:T(8,128)(2,1)} %get-tuple-element.28., ...), custom_call_target="tpu_custom_call" | custom-call | tf_op jit(solution)/shard_map/finish/pallas_call | solution.py:886

commit v5 on v4

--- a/solution.py
+++ b/solution.py
@@ -145,6 +145,7 @@
         size = jnp.maximum(pre, 0.0) + jnp.log1p(jnp.exp(-jnp.abs(pre)))
         s.step[:, cols] = size
         s.sigp[:, cols] = jax.nn.sigmoid(pre)
+        s.drive[:, cols] = size * s.active[:, cols].astype(F32)
 
     repeat(s.E // 256, run, 6)
     s.decay[...] = -jnp.exp(s.small[pl.ds(0, s.N), :]) * LOG2E
@@ -162,8 +163,7 @@
     def run(block, state):
         scan_sum(jnp.maximum(block - 1, 0))
         rows = span(block, STEPS)
-        size = s.step[rows, :]
-        push = size * s.active[rows, :].astype(F32)
+        size, push = s.step[rows, :], s.drive[rows, :]
         for i in range(STEPS):
             t = block * STEPS + i
             b_row = s.spread[span(t, N), pl.ds(0, 128)]
@@ -254,8 +254,7 @@
             held = s.lam[:, cols]
             s.gact[rows, cols] = dot(s.bmat[rows, :], held)
             s.gslope[rows, cols] = dot(gather, s.part[:, cols])
-            drive = (size * s.active[rows, cols].astype(F32)).astype(BF16)
-            b_part = dot(drive, held, (1, 1))
+            b_part = dot(s.drive[rows, cols].astype(BF16), held, (1, 1))
             after = s.states[pl.ds(pl.multiple_of(block * wide + N, N), wide), cols]
             c_part = dot(d_value.astype(BF16), after, (1, 1))
             if chunk == 0:
@@ -280,7 +279,7 @@
         adjoint = s.gact[:, cols]
         d_pre = (wide * adjoint + s.gslope[:, cols] * (1.0 / LOG2E)) * s.sigp[:, cols]
         s.rows[pl.ds(at.dt_bias, 1), cols] = jnp.sum(d_pre, axis=0, keepdims=True)
-        s.d_pre_low[:, cols] = d_pre.astype(BF16)
+        s.lam[:, cols] = d_pre.astype(BF16)
         s.d_mixed[:, cols] = (
             s.d_mixed[:, cols] * s.small[pl.ds(at.skip, 1), cols] + s.step[:, cols] * adjoint
         )
@@ -294,7 +293,7 @@
     col = lax.broadcasted_iota(jnp.int32, (wide, s.N), 1)
     pick = (row % s.N == col).astype(BF16)
     mask = diagonal(s)
-    s.d_proj[:, pl.ds(0, s.R)] = dot(s.d_pre_low[...], s.w_dt[...], (1, 1)).astype(BF16)
+    s.d_proj[:, pl.ds(0, s.R)] = dot(s.lam[...], s.w_dt[...], (1, 1)).astype(BF16)
     s.d_proj[:, pl.ds(s.R, s.N)] = dot((s.db[...] * mask).astype(BF16), pick).astype(BF16)
     s.d_proj[:, pl.ds(s.R + s.N, s.N)] = dot((s.dc[...] * mask).astype(BF16), pick).astype(BF16)
 
@@ -306,7 +305,7 @@
 
     def run(index):
         cols = span(part + index, 128)
-        s.rows[pl.ds(first, s.R), cols] = dot(s.proj[:, : s.R], s.d_pre_low[:, cols], (0, 0))
+        s.rows[pl.ds(first, s.R), cols] = dot(s.proj[:, : s.R], s.lam[:, cols], (0, 0))
         s.rows[pl.ds(first + s.R, s.J), cols] = dot(s.d_proj[...], s.active[:, cols], (0, 0))
         d_active = s.d_mixed[:, cols] + dot(s.d_proj[...], s.w_xt[:, cols])
         d_value = d_active * s.cslope[:, cols]
@@ -321,13 +320,13 @@
             total = total + taps * s.mixed[pl.ds(s.K - 1 - k, s.T), cols]
         s.d_inner[:, cols] = total.astype(BF16)
 
-    repeat(count, run, 6)
+    repeat(count, run, 3)
 
 
 def back_in(s):
     def run(index):
         rows = span(index, 256)
-        s.d_normed[:, rows] = dot(s.d_inner[...], s.w_in[rows, pl.ds(0, s.E)], (1, 1)) + dot(
+        s.step[:, rows] = dot(s.d_inner[...], s.w_in[rows, pl.ds(0, s.E)], (1, 1)) + dot(
             s.d_gate[...], s.w_in[rows, pl.ds(s.E, s.E)], (1, 1)
         )
 
@@ -341,7 +340,7 @@
         rows = span(block, 64)
         x = s.tok[rows, :].astype(F32)
         scale = s.inv[rows, pl.ds(0, 1)]
-        d_value = s.d_normed[rows, :]
+        d_value = s.step[rows, pl.ds(0, s.D)]
         s.d_gain[...] += jnp.sum(d_value * x * scale, axis=0, keepdims=True)
         d_scaled = d_value * s.gain[...]
         shared = jnp.mean(d_scaled * x, axis=1, keepdims=True)
@@ -368,10 +367,10 @@
     return dict(
         inv=((T, 128), F32), gain=((1, D), F32), small=((count, E), F32), inner=padded, gact=full, gslope=full,
         cslope=full, active=low, proj=((T, J), BF16), bmat=((T, wide), BF16), cmat=((T, wide), BF16),
-        spread=((T * N, 256), F32), decay=((N, E), F32), step=full, sigp=full,
+        spread=((T * N, 256), F32), decay=((N, E), F32), step=full, sigp=full, drive=full,
         mixed=padded, d_mixed=full, states=(((T + 1) * N, E), BF16), carry=((N, E), F32),
         lam=((wide, E), BF16), part=((wide // 2, E), BF16), db=((T, wide), F32), dc=((T, wide), F32),
-        d_pre_low=low, d_proj=((T, J), BF16), d_normed=((T, D), F32), d_gain=((1, D), F32),
+        d_proj=((T, J), BF16), d_gain=((1, D), F32),
     )
 
 
@@ -451,36 +450,36 @@
 
 
 ORDERS = (
-    ((3,), (0,), (1,), (2,)),
+    ((2,), (0,), (3,), (1,)),
+    ((0, 1), (2, 3)),
+    ((1,), (0,), (2, 3)),
+    ((1,), (0,), (2, 3)),
     ((2,), (1,), (0,), (3,)),
-    ((0,), (2,), (1,), (3,)),
-    ((0, 1), (2, 3)),
-    ((0,), (1,), (2,), (3,)),
-    ((1,), (0,), (2,), (3,)),
+    ((0,), (1,), (2, 3)),
+    ((0,), (1,), (2, 3)),
     ((1,), (0,), (2, 3)),
-    ((0,), (1,), (2, 3)),
     ((2,), (0, 1), (3,)),
-    ((1,), (0,), (2, 3)),
+    ((0, 1), (3,), (2,)),
 )
 DURING = {
-    6: ((2, 0),),
-    9: ((0, 0), (1, 0), (3, 0)),
-    11: ((2, 1), (5, 0)),
-    13: ((3, 1), (4, 0), (1, 1)),
-    14: ((2, 2),),
-    15: ((0, 1),),
-    17: ((5, 1), (4, 1), (3, 2)),
-    18: ((2, 3), (1, 2), (0, 2)),
-    19: ((5, 2),),
-    20: ((4, 2),),
-    21: ((2, 4),),
-    22: ((1, 3), (0, 3), (3, 3)),
+    6: ((0, 0), (1, 0)),
+    9: ((4, 0),),
+    10: ((2, 0), (5, 0)),
+    11: ((1, 1), (0, 1)),
+    13: ((3, 0),),
+    14: ((2, 1),),
+    15: ((4, 1), (1, 2)),
+    16: ((5, 1), (0, 2), (3, 1)),
+    18: ((4, 2), (2, 2)),
+    19: ((5, 2), (0, 3), (1, 3)),
+    20: ((3, 2),),
+    21: ((4, 3),),
 }
 AFTER = (
-    (5, 3), (6, 0), (7, 0), (8, 0), (2, 5), (4, 3), (0, 4), (1, 4), (5, 4), (6, 1), (9, 0), (2, 6),
-    (7, 1), (4, 4), (5, 5), (1, 5), (8, 1), (9, 1), (6, 2), (0, 5), (7, 2), (4, 5), (1, 6), (8, 2),
-    (2, 7), (9, 2), (4, 6), (5, 6), (6, 3), (0, 6), (7, 3), (1, 7), (5, 7), (8, 3), (4, 7), (9, 3),
-    (7, 4), (6, 4), (8, 4), (9, 4), (6, 5), (0, 7), (7, 5), (8, 5), (9, 5),
+    (0, 4), (2, 3), (6, 0), (5, 3), (7, 0), (8, 0), (9, 0), (3, 3), (2, 4), (4, 4), (6, 1), (7, 1),
+    (0, 5), (5, 4), (9, 1), (8, 1), (3, 4), (6, 2), (4, 5), (9, 2), (7, 2), (8, 2), (0, 6), (2, 5),
+    (9, 3), (6, 3), (5, 5), (7, 3), (3, 5), (8, 3), (4, 6), (7, 4), (0, 7), (6, 4), (9, 4), (8, 4),
+    (4, 7), (6, 5), (7, 5), (8, 5), (9, 5),
 )
 PIECES = 16
 FIRST, SECOND = 0, 2
@@ -743,12 +742,13 @@
     back_conv(s, 6, 6)
     swaps[5].start()
     carry_on(DURING.get(18, ()))
-    phase(19, back_in)
     for color in range(3):
         if color < 2:
             swaps[4 + color].wait_recv()
         grad_in(2, color, s.d_inner, s.d_inner_in)
         units[6 + color].start()
+        if color == 0:
+            phase(19, back_in)
     carry_on(DURING.get(20, ()))
     back_norm(s)
     s.rows[pl.ds(at.gain, 1), pl.ds(0, DH)] = s.d_gain[:, pl.ds(0, DH)]

time: 102 us -> 100 us (0.980)
  Pallas kernels: 99.8 us -> 98.4 us
    pallas_call x1, Pallas kernels: 95 us -> 93.5 us  [fused_layer(): pl.pallas_call(functools.partial(fused_kernel, z, names), out_shape=[jax....]
where the time goes in v5:
time: 100 us; the launch traced here: 99.8 us
  Pallas kernels  98.4 us (98%)
  between operations  1.46 us (1%)
    pallas_call x1, Pallas kernels, fused_layer(): pl.pallas_call(functools.partial(fused_kernel, z, names), out_shape=[jax....  93.5 us
    pallas_call x1, Pallas kernels, fused_body(): pl.pallas_call(functools.partial(finish_kernel, a_log.shape[0], conv_w.sh...  4.84 us

profile of v5, /device:TPU:0, one launch (start us, length us, event | category | flops | bytes accessed | tf_op | source)
XLA Modules:
  0.0 99.8 jit_solution(14127965955033333951)
XLA Ops:
  1.3 93.5 %layer.1 = (bf16[256,768]{1,0:T(8,128)(2,1)}, f32[256,768]{1,0:T(8,128)}, bf16[2304,768]{1,0:T(8,128)(2,1)}, bf16[512,256]{1,0:T(8,128)(2,1)}) custom-call(s32[1]{0:T(128)S(6)} %copy.25.refs_0_, bf16[256,768]{1,0:T(8,128)(2,1)} %bitcast.6, bf16[256,768]{1,0:T(8,128)(2,1)} %bitcast.7, bf16[384]{0:T(512)(128)(2,1)} %refs_3_.1, bf16[384,3072]{1,0:T(8,128)(2,1)} %refs_4_.1, ...), custom_call_target="tpu_custom_call" | custom-call | tf_op jit(solution)/shard_map/layer/pallas_call | solution.py:806
  94.8 4.8 %finish.1 = (bf16[256,768]{1,0:T(8,128)(2,1)}, f32[256,768]{1,0:T(8,128)}, f32[384]{0:T(512)}, f32[384,3072]{1,0:T(8,128)}, f32[4,768]{1,0:T(4,128)}, /*index=5*...) custom-call(bf16[2304,768]{1,0:T(8,128)(2,1)} %get-tuple-element.28., ...), custom_call_target="tpu_custom_call" | custom-call | tf_op jit(solution)/shard_map/finish/pallas_call | solution.py:886

commit v6 on v5

--- a/solution.py
+++ b/solution.py
@@ -476,10 +476,10 @@
     21: ((4, 3),),
 }
 AFTER = (
-    (0, 4), (2, 3), (6, 0), (5, 3), (7, 0), (8, 0), (9, 0), (3, 3), (2, 4), (4, 4), (6, 1), (7, 1),
-    (0, 5), (5, 4), (9, 1), (8, 1), (3, 4), (6, 2), (4, 5), (9, 2), (7, 2), (8, 2), (0, 6), (2, 5),
-    (9, 3), (6, 3), (5, 5), (7, 3), (3, 5), (8, 3), (4, 6), (7, 4), (0, 7), (6, 4), (9, 4), (8, 4),
-    (4, 7), (6, 5), (7, 5), (8, 5), (9, 5),
+    (6, 0), (0, 4), (2, 3), (7, 0), (8, 0), (5, 3), (9, 0), (3, 3), (6, 1), (2, 4), (7, 1), (4, 4),
+    (9, 1), (0, 5), (8, 1), (5, 4), (6, 2), (3, 4), (9, 2), (7, 2), (4, 5), (8, 2), (9, 3), (0, 6),
+    (6, 3), (2, 5), (7, 3), (5, 5), (8, 3), (3, 5), (7, 4), (4, 6), (6, 4), (9, 4), (0, 7), (8, 4),
+    (6, 5), (7, 5), (4, 7), (8, 5), (9, 5),
 )
 PIECES = 16
 FIRST, SECOND = 0, 2

time: 100 us -> 99.6 us (level)
  no operation moved by 1% of the time
where the time goes in v6:
time: 99.6 us; the launch traced here: 99.4 us
  Pallas kernels  98 us (98%)
  between operations  1.46 us (1%)
    pallas_call x1, Pallas kernels, fused_layer(): pl.pallas_call(functools.partial(fused_kernel, z, names), out_shape=[jax....  93.1 us
    pallas_call x1, Pallas kernels, fused_body(): pl.pallas_call(functools.partial(finish_kernel, a_log.shape[0], conv_w.sh...  4.84 us

profile of v6, /device:TPU:0, one launch (start us, length us, event | category | flops | bytes accessed | tf_op | source)
XLA Modules:
  0.0 99.4 jit_solution(14458072284413773614)
XLA Ops:
  1.3 93.1 %layer.1 = (bf16[256,768]{1,0:T(8,128)(2,1)}, f32[256,768]{1,0:T(8,128)}, bf16[2304,768]{1,0:T(8,128)(2,1)}, bf16[512,256]{1,0:T(8,128)(2,1)}) custom-call(s32[1]{0:T(128)S(6)} %copy.25.refs_0_, bf16[256,768]{1,0:T(8,128)(2,1)} %bitcast.6, bf16[256,768]{1,0:T(8,128)(2,1)} %bitcast.7, bf16[384]{0:T(512)(128)(2,1)} %refs_3_.1, bf16[384,3072]{1,0:T(8,128)(2,1)} %refs_4_.1, ...), custom_call_target="tpu_custom_call" | custom-call | tf_op jit(solution)/shard_map/layer/pallas_call | solution.py:806
  94.4 4.8 %finish.1 = (bf16[256,768]{1,0:T(8,128)(2,1)}, f32[256,768]{1,0:T(8,128)}, f32[384]{0:T(512)}, f32[384,3072]{1,0:T(8,128)}, f32[4,768]{1,0:T(4,128)}, /*index=5*...) custom-call(bf16[2304,768]{1,0:T(8,128)(2,1)} %get-tuple-element.28., ...), custom_call_target="tpu_custom_call" | custom-call | tf_op jit(solution)/shard_map/finish/pallas_call | solution.py:886
